TPU v7x, 32 devices: a whole 2x2x4 slice. The times are simulated.
32 devices in a mesh: mpo: 4 (over y, core), blk: 8 (over z, x).
Axes of the slice: x: 2, y: 2, z: 4, core: 2. Of those that a mesh axis runs over, the one named last changes fastest.
Arguments:
- two_site: bfloat16 [64, 16, 128, 128], P('blk'), may hold values from -6 to 6
- left_env: bfloat16 [34, 64, 128, 128], P(None, 'blk'), may hold values from -0.5 to 0.5
- right_env: bfloat16 [34, 64, 128, 128], P(None, 'blk'), may hold values from -0.5 to 0.5
- mpo_terms: bfloat16 [32, 16, 16], P('mpo'), may hold values from -0.25 to 0.25
- term_left: int32 [32], P('mpo'), may hold values from 0 to 33
- term_right: int32 [32], P('mpo'), may hold values from 0 to 33
- shifts: int32 [16], replicated, may hold values from -1 to 1, as said below
- block_sizes: int32 [64], replicated, may hold values from 64 to 128, as said below
Outputs:
- applied: bfloat16 [64, 16, 128, 128], P('blk', 'mpo')
Inputs may be any that keep to these rules, and one draw needn't show every extreme that they name: `shifts`: both -1 and 1 occur among the offsets. `block_sizes`: both 128 // 2 and 128 occur among the live dimensions.
All inputs are finite; a program needn't handle non-finite values.
Results may differ from a plain program's by a relative error of at most 0.0057.
Values may be sent and summed in bfloat16 or wider, within the bound.
No kernel may reach another device: no remote copies, remote signals or barrier semaphores. Data moves between devices by JAX's collectives and lax.ppermute only.
A program may use at most 128 MiB of HBM per device.

v0:
```python
import jax
import jax.numpy as jnp
from jax import lax
from jax.sharding import PartitionSpec as P

SH = 1


def with_halo(cells, sides, width):
    for axis, dim in sides:
        count = lax.axis_size(axis)
        ends = count - 1
        head = lax.slice_in_dim(cells, 0, width, axis=dim)
        tail = lax.slice_in_dim(cells, cells.shape[dim] - width, cells.shape[dim], axis=dim)
        cells = jnp.concatenate(
            [
                lax.ppermute(tail, axis, [(i, (i + 1) % count) for i in range(ends)]),
                cells,
                lax.ppermute(head, axis, [((i + 1) % count, i) for i in range(ends)]),
            ],
            axis=dim,
        )
    return cells


def sector_mask(block_sizes, shifts, first, blocks, total, depth):
    rows_left = first + jnp.arange(blocks, dtype=jnp.int32)
    right_index = rows_left[:, None] + shifts[None, :]
    inside = (right_index >= 0) & (right_index < total)
    table = jnp.arange(total, dtype=jnp.int32)
    size_left = jnp.sum(
        jnp.where(rows_left[:, None] == table[None, :], block_sizes[None, :], 0), axis=1
    )
    size_right = jnp.sum(
        jnp.where(right_index[:, :, None] == table[None, None, :], block_sizes[None, None, :], 0),
        axis=2,
    )
    lines = jnp.arange(depth, dtype=jnp.int32)
    keep_rows = lines[None, None, :, None] < size_left[:, None, None, None]
    keep_cols = lines[None, None, None, :] < size_right[:, :, None, None]
    return keep_rows & keep_cols & inside[:, :, None, None]


def body(two_site, left_env, right_env, mpo_terms, term_left, term_right, shifts, block_sizes):
    blocks = two_site.shape[0]
    depth = two_site.shape[2]
    total = blocks * lax.axis_size("blk")
    first = lax.axis_index("blk") * blocks
    mask = sector_mask(block_sizes, shifts, first, blocks, total, depth)
    clean = jnp.where(mask, two_site, jnp.zeros_like(two_site))
    chosen = jnp.take(right_env, term_right, axis=0)
    padded = with_halo(chosen, (("blk", 1),), SH)
    picked = jnp.arange(term_right.shape[0], dtype=jnp.int32)
    starts = shifts + SH

    def one_term(summed, item):
        left_index, right_index, matrix = item
        left_block = lax.dynamic_index_in_dim(left_env, left_index, 0, keepdims=False)
        applied_left = jnp.einsum(
            "bxy,bqyz->bqxz", left_block, clean, preferred_element_type=jnp.float32
        ).astype(jnp.bfloat16)
        mixed = jnp.einsum(
            "pq,bqxz->bpxz", matrix, applied_left, preferred_element_type=jnp.float32
        )
        mixed_half = mixed.astype(jnp.bfloat16)
        right_rows = lax.dynamic_index_in_dim(padded, right_index, 0, keepdims=False)
        gathered = jax.vmap(lambda begin: lax.dynamic_slice_in_dim(right_rows, begin, blocks, 0))(
            starts
        )
        product = jnp.einsum(
            "bpxz,pbzy->bpxy", mixed_half, gathered, preferred_element_type=jnp.float32
        )
        return (summed + product, None)

    summed, unused = lax.scan(
        one_term, jnp.zeros(two_site.shape, jnp.float32), (term_left, picked, mpo_terms)
    )
    masked = jnp.where(mask, summed, jnp.float32(0.0))
    return lax.psum_scatter(masked, "mpo", scatter_dimension=1, tiled=True).astype(jnp.bfloat16)


def solution(mesh):
    return jax.shard_map(
        body,
        mesh=mesh,
        in_specs=(
            P("blk", None, None, None),
            P(None, "blk", None, None),
            P(None, "blk", None, None),
            P("mpo", None, None),
            P("mpo"),
            P("mpo"),
            P(),
            P(),
        ),
        out_specs=P("blk", "mpo", None, None),
        check_vma=False,
    )
```

profile of v0, /device:TPU:0, one launch (start us, length us, event | category | flops | bytes accessed | tf_op | source)
XLA Modules:
  0.0 406.9 jit_solution(6340689314098448103)
XLA Ops:
  1.4 5.7 %gather_fusion.1 = bf16[8,8,128,128]{3,2,1,0:T(8,128)(2,1)} fusion(bf16[34,8,128,128]{3,2,1,0:T(8,128)(2,1)} %param.12, s32[1024]{0:T(1024)S(1)} %pad_clamp_fusion), kind=kCustom, calls=%fused_computation.1 | custom fusion | bytes 4194336 | tf_op jit(solution)/shard_map/jit(_take)/gather | solution.py:51
  9.0 4.9 %collective-permute-start = (bf16[8,1,128,128]{3,2,1,0:T(8,128)(2,1)S(1)}, bf16[8,1,128,128]{3,2,1,0:T(8,128)(2,1)S(1)}, u32[]{:S(2)}, u32[]{:S(2)}) collective-permute-start(bf16[8,1,128,128]{3,2,1,0:T(8,128)(2,1)S(1)} %get-tuple-element.101), channel_id=1, source_target_pairs={{0,1},{1,2},{2,3},{3,4},{4,5},{5,6},{6,7},{8,9},{9,10},{10,11},{11... | collective-permute-start | bytes 786440 | tf_op jit(solution)/shard_map/ppermute | solution.py:17
  15.9 5.0 %fusion.21 = bf16[8,16,128,128]{3,2,1,0:T(8,128)(2,1)} fusion(bf16[8,16,128,128]{3,2,1,0:T(8,128)(2,1)} %param.10, pred[8,16]{1,0:T(8,128)(4,1)S(1)} %compare_and_fusion, pred[8,16,128]{2,1,0:T(8,128)(4,1)S(1)} %iota_compare_fusion.1, pred[8,128]{1,0:T(8,128)(4,1)S(1)} %iota_compare_fusion.3), kind=kLoop, calls=%fused_computation.23 | loop fusion | flops 6291456 | bytes 8406144 | tf_op jit(solution)/shard_map/jit(_where)/select_n | solution.py:50
  26.8 225.2 %while.11 = (s32[]{:T(128)}, f32[8,16,128,128]{3,2,1,0:T(8,128)}, s32[8]{0:T(128)S(1)}, bf16[34,8,128,128]{3,2,1,0:T(8,128)(2,1)}, bf16[8,16,128,128]{3,2,1,0:T(...) while((s32[]{:T(128)}, f32[8,16,128,128]{3,2,1,0:T(8,128)}, ...), condition=%wide.region_3.4_spmd.clone, body=%wide.region_2.3_spmd.clone.sunk | while | flops 1149239296 | bytes 51254312 | solution.py:75
  29.3 3.5 convert_bitcast_fusion.4
  32.8 5.4 %convert_bitcast_fusion.5 = bf16[8,16,128,128]{3,1,2,0:T(8,128)(2,1)} fusion(bf16[8,16,128,128]{3,2,1,0:T(8,128)(2,1)S(1)} %convert_bitcast_fusion.4, bf16[8,16,16]{2,1,0:T(8,128)(2,1)} %get-tuple-element.189, s32[]{:T(128)} %get-tuple-element.171), kind=kOutput, calls=%fused_computation.8.clone.1 | convolution fusion | flops 69206016 | bytes 8393216 | tf_op jit(solution)/shard_map/while/body/eval_jaxpr/pq,bqxz->bpxz/dot_general | solution.py:62
  44.5 8.4 %select_add_fusion.2 = f32[8,16,128,128]{3,2,1,0:T(8,128)} fusion(f32[8,16,128,128]{3,2,1,0:T(8,128)} %get-tuple-element.172, pred[]{:T(512)S(6)} %compare.4, bf16[16,8,128,128]{3,2,1,0:T(8,128)(2,1)} %gather_fusion, bf16[8,16,128,128]{3,1,2,0:T(8,128)(2,1)} %convert_bitcast_fusion.5), kind=kOutput, calls=%fused_computation.2.clone.1 | convolution fusion | flops 541065216 | bytes 25165824 | tf_op jit(solution)/shard_map/while/body/eval_jaxpr/bpxz,pbzy->bpxy/dot_general | solution.py:70
  58.9 5.4 %convert_bitcast_fusion.5 = bf16[8,16,128,128]{3,1,2,0:T(8,128)(2,1)} fusion(bf16[8,16,128,128]{3,2,1,0:T(8,128)(2,1)S(1)} %convert_bitcast_fusion.4, bf16[8,16,16]{2,1,0:T(8,128)(2,1)} %get-tuple-element.189, s32[]{:T(128)} %get-tuple-element.171), kind=kOutput, calls=%fused_computation.8.clone.1 | convolution fusion | flops 69206016 | bytes 8393216 | tf_op jit(solution)/shard_map/while/body/eval_jaxpr/pq,bqxz->bpxz/dot_general | solution.py:62
  70.6 10.8 %select_add_fusion.2 = f32[8,16,128,128]{3,2,1,0:T(8,128)} fusion(f32[8,16,128,128]{3,2,1,0:T(8,128)} %get-tuple-element.172, pred[]{:T(512)S(6)} %compare.4, bf16[16,8,128,128]{3,2,1,0:T(8,128)(2,1)} %gather_fusion, bf16[8,16,128,128]{3,1,2,0:T(8,128)(2,1)} %convert_bitcast_fusion.5), kind=kOutput, calls=%fused_computation.2.clone.1 | convolution fusion | flops 541065216 | bytes 25165824 | tf_op jit(solution)/shard_map/while/body/eval_jaxpr/bpxz,pbzy->bpxy/dot_general | solution.py:70
  87.3 5.4 %convert_bitcast_fusion.5 = bf16[8,16,128,128]{3,1,2,0:T(8,128)(2,1)} fusion(bf16[8,16,128,128]{3,2,1,0:T(8,128)(2,1)S(1)} %convert_bitcast_fusion.4, bf16[8,16,16]{2,1,0:T(8,128)(2,1)} %get-tuple-element.189, s32[]{:T(128)} %get-tuple-element.171), kind=kOutput, calls=%fused_computation.8.clone.1 | convolution fusion | flops 69206016 | bytes 8393216 | tf_op jit(solution)/shard_map/while/body/eval_jaxpr/pq,bqxz->bpxz/dot_general | solution.py:62
  99.0 10.8 %select_add_fusion.2 = f32[8,16,128,128]{3,2,1,0:T(8,128)} fusion(f32[8,16,128,128]{3,2,1,0:T(8,128)} %get-tuple-element.172, pred[]{:T(512)S(6)} %compare.4, bf16[16,8,128,128]{3,2,1,0:T(8,128)(2,1)} %gather_fusion, bf16[8,16,128,128]{3,1,2,0:T(8,128)(2,1)} %convert_bitcast_fusion.5), kind=kOutput, calls=%fused_computation.2.clone.1 | convolution fusion | flops 541065216 | bytes 25165824 | tf_op jit(solution)/shard_map/while/body/eval_jaxpr/bpxz,pbzy->bpxy/dot_general | solution.py:70
  112.2 3.5 convert_bitcast_fusion.4
  115.7 5.4 %convert_bitcast_fusion.5 = bf16[8,16,128,128]{3,1,2,0:T(8,128)(2,1)} fusion(bf16[8,16,128,128]{3,2,1,0:T(8,128)(2,1)S(1)} %convert_bitcast_fusion.4, bf16[8,16,16]{2,1,0:T(8,128)(2,1)} %get-tuple-element.189, s32[]{:T(128)} %get-tuple-element.171), kind=kOutput, calls=%fused_computation.8.clone.1 | convolution fusion | flops 69206016 | bytes 8393216 | tf_op jit(solution)/shard_map/while/body/eval_jaxpr/pq,bqxz->bpxz/dot_general | solution.py:62
  127.5 10.8 %select_add_fusion.2 = f32[8,16,128,128]{3,2,1,0:T(8,128)} fusion(f32[8,16,128,128]{3,2,1,0:T(8,128)} %get-tuple-element.172, pred[]{:T(512)S(6)} %compare.4, bf16[16,8,128,128]{3,2,1,0:T(8,128)(2,1)} %gather_fusion, bf16[8,16,128,128]{3,1,2,0:T(8,128)(2,1)} %convert_bitcast_fusion.5), kind=kOutput, calls=%fused_computation.2.clone.1 | convolution fusion | flops 541065216 | bytes 25165824 | tf_op jit(solution)/shard_map/while/body/eval_jaxpr/bpxz,pbzy->bpxy/dot_general | solution.py:70
  144.2 5.4 %convert_bitcast_fusion.5 = bf16[8,16,128,128]{3,1,2,0:T(8,128)(2,1)} fusion(bf16[8,16,128,128]{3,2,1,0:T(8,128)(2,1)S(1)} %convert_bitcast_fusion.4, bf16[8,16,16]{2,1,0:T(8,128)(2,1)} %get-tuple-element.189, s32[]{:T(128)} %get-tuple-element.171), kind=kOutput, calls=%fused_computation.8.clone.1 | convolution fusion | flops 69206016 | bytes 8393216 | tf_op jit(solution)/shard_map/while/body/eval_jaxpr/pq,bqxz->bpxz/dot_general | solution.py:62
  155.9 10.8 %select_add_fusion.2 = f32[8,16,128,128]{3,2,1,0:T(8,128)} fusion(f32[8,16,128,128]{3,2,1,0:T(8,128)} %get-tuple-element.172, pred[]{:T(512)S(6)} %compare.4, bf16[16,8,128,128]{3,2,1,0:T(8,128)(2,1)} %gather_fusion, bf16[8,16,128,128]{3,1,2,0:T(8,128)(2,1)} %convert_bitcast_fusion.5), kind=kOutput, calls=%fused_computation.2.clone.1 | convolution fusion | flops 541065216 | bytes 25165824 | tf_op jit(solution)/shard_map/while/body/eval_jaxpr/bpxz,pbzy->bpxy/dot_general | solution.py:70
  172.6 5.4 %convert_bitcast_fusion.5 = bf16[8,16,128,128]{3,1,2,0:T(8,128)(2,1)} fusion(bf16[8,16,128,128]{3,2,1,0:T(8,128)(2,1)S(1)} %convert_bitcast_fusion.4, bf16[8,16,16]{2,1,0:T(8,128)(2,1)} %get-tuple-element.189, s32[]{:T(128)} %get-tuple-element.171), kind=kOutput, calls=%fused_computation.8.clone.1 | convolution fusion | flops 69206016 | bytes 8393216 | tf_op jit(solution)/shard_map/while/body/eval_jaxpr/pq,bqxz->bpxz/dot_general | solution.py:62
  184.4 10.8 %select_add_fusion.2 = f32[8,16,128,128]{3,2,1,0:T(8,128)} fusion(f32[8,16,128,128]{3,2,1,0:T(8,128)} %get-tuple-element.172, pred[]{:T(512)S(6)} %compare.4, bf16[16,8,128,128]{3,2,1,0:T(8,128)(2,1)} %gather_fusion, bf16[8,16,128,128]{3,1,2,0:T(8,128)(2,1)} %convert_bitcast_fusion.5), kind=kOutput, calls=%fused_computation.2.clone.1 | convolution fusion | flops 541065216 | bytes 25165824 | tf_op jit(solution)/shard_map/while/body/eval_jaxpr/bpxz,pbzy->bpxy/dot_general | solution.py:70
  201.1 5.4 %convert_bitcast_fusion.5 = bf16[8,16,128,128]{3,1,2,0:T(8,128)(2,1)} fusion(bf16[8,16,128,128]{3,2,1,0:T(8,128)(2,1)S(1)} %convert_bitcast_fusion.4, bf16[8,16,16]{2,1,0:T(8,128)(2,1)} %get-tuple-element.189, s32[]{:T(128)} %get-tuple-element.171), kind=kOutput, calls=%fused_computation.8.clone.1 | convolution fusion | flops 69206016 | bytes 8393216 | tf_op jit(solution)/shard_map/while/body/eval_jaxpr/pq,bqxz->bpxz/dot_general | solution.py:62
  212.8 10.8 %select_add_fusion.2 = f32[8,16,128,128]{3,2,1,0:T(8,128)} fusion(f32[8,16,128,128]{3,2,1,0:T(8,128)} %get-tuple-element.172, pred[]{:T(512)S(6)} %compare.4, bf16[16,8,128,128]{3,2,1,0:T(8,128)(2,1)} %gather_fusion, bf16[8,16,128,128]{3,1,2,0:T(8,128)(2,1)} %convert_bitcast_fusion.5), kind=kOutput, calls=%fused_computation.2.clone.1 | convolution fusion | flops 541065216 | bytes 25165824 | tf_op jit(solution)/shard_map/while/body/eval_jaxpr/bpxz,pbzy->bpxy/dot_general | solution.py:70
  229.5 5.4 %convert_bitcast_fusion.5 = bf16[8,16,128,128]{3,1,2,0:T(8,128)(2,1)} fusion(bf16[8,16,128,128]{3,2,1,0:T(8,128)(2,1)S(1)} %convert_bitcast_fusion.4, bf16[8,16,16]{2,1,0:T(8,128)(2,1)} %get-tuple-element.189, s32[]{:T(128)} %get-tuple-element.171), kind=kOutput, calls=%fused_computation.8.clone.1 | convolution fusion | flops 69206016 | bytes 8393216 | tf_op jit(solution)/shard_map/while/body/eval_jaxpr/pq,bqxz->bpxz/dot_general | solution.py:62
  241.3 10.8 %select_add_fusion.2 = f32[8,16,128,128]{3,2,1,0:T(8,128)} fusion(f32[8,16,128,128]{3,2,1,0:T(8,128)} %get-tuple-element.172, pred[]{:T(512)S(6)} %compare.4, bf16[16,8,128,128]{3,2,1,0:T(8,128)(2,1)} %gather_fusion, bf16[8,16,128,128]{3,1,2,0:T(8,128)(2,1)} %convert_bitcast_fusion.5), kind=kOutput, calls=%fused_computation.2.clone.1 | convolution fusion | flops 541065216 | bytes 25165824 | tf_op jit(solution)/shard_map/while/body/eval_jaxpr/bpxz,pbzy->bpxy/dot_general | solution.py:70
  252.0 6.4 %fusion.20 = f32[8,16,128,128]{3,2,1,0:T(8,128)} fusion(f32[8,16,128,128]{3,2,1,0:T(8,128)} %get-tuple-element.52, pred[8,16]{1,0:T(8,128)(4,1)S(1)} %compare_and_fusion, pred[8,16,128]{2,1,0:T(8,128)(4,1)S(1)} %iota_compare_fusion.1, pred[8,128]{1,0:T(8,128)(4,1)S(1)} %iota_compare_fusion.3), kind=kLoop, calls=%fused_computation.22 | loop fusion | flops 6291456 | bytes 16794752 | tf_op jit(solution)/shard_map/jit(_where)/select_n | solution.py:78
  258.5 146.1 %all-reduce.3 = bf16[8,16,128,128]{3,2,1,0:T(8,128)(2,1)} all-reduce(f32[8,16,128,128]{3,2,1,0:T(8,128)} %fusion.20), channel_id=2, replica_groups=mesh['mpo'=4,'blk'=8] {'mpo'}, use_global_device_ids=true, to_apply=%region_4.5.clone | all-reduce | flops 2097152 | bytes 12582912
  (75 shorter events, 75.6 us)
Async XLA Ops:
  1.3 13.8 %copy-start = (s32[16]{0:T(128)S(1)}, s32[16]{0:T(128)}, u32[]{:S(2)}) copy-start(s32[16]{0:T(128)} %param.16) | copy-start | bytes 196
  1.3 14.0 %copy-start.1 = (s32[64]{0:T(128)S(1)}, s32[64]{0:T(128)}, u32[]{:S(2)}) copy-start(s32[64]{0:T(128)} %param.17) | copy-start | bytes 772
  9.0 16.0 %collective-permute-start = (bf16[8,1,128,128]{3,2,1,0:T(8,128)(2,1)S(1)}, bf16[8,1,128,128]{3,2,1,0:T(8,128)(2,1)S(1)}, u32[]{:S(2)}, u32[]{:S(2)}) collective-permute-start(bf16[8,1,128,128]{3,2,1,0:T(8,128)(2,1)S(1)} %get-tuple-element.101), channel_id=1, source_target_pairs={{0,1},{1,2},{2,3},{3,4},{4,5},{5,6},{6,7},{8,9},{9,10},{10,11},{11... | collective-permute-start | bytes 786440 | tf_op jit(solution)/shard_map/ppermute | solution.py:17
  13.8 11.2 %collective-permute-start.1 = (bf16[8,1,128,128]{3,2,1,0:T(8,128)(2,1)S(1)}, bf16[8,1,128,128]{3,2,1,0:T(8,128)(2,1)S(1)}, u32[]{:S(2)}, u32[]{:S(2)}) collective-permute-start(bf16[8,1,128,128]{3,2,1,0:T(8,128)(2,1)S(1)} %get-tuple-element.102), channel_id=1, source_target_pairs={{1,0},{2,1},{3,2},{4,3},{5,4},{6,5},{7,6},{9,8},{10,9},{11,10},{12... | collective-permute-start | bytes 786440 | tf_op jit(solution)/shard_map/ppermute | solution.py:19
  15.9 5.0 %copy-start.3 = (u32[32]{0:T(128)S(1)}, u32[32]{0:T(128)}, u32[]{:S(2)}) copy-start(u32[32]{0:T(128)} %constant.88) | copy-start | bytes 388
  21.0 5.9 %copy-start.2 = (s32[8]{0:T(128)S(1)}, s32[8]{0:T(128)}, u32[]{:S(2)}) copy-start(s32[8]{0:T(128)} %param.14) | copy-start | bytes 100
where the time goes:
time: 411 us; the launch traced here: 407 us
  matrix products  155 us (38%)
  blocking collectives  146 us (36%)
  local copies, waits for them, and re-layouts  50.3 us (12%)
  loops' own time  28.2 us (7%)
  other arithmetic  17.3 us (4%)
  starting transfers between devices  6.15 us (1%)
    unnamed x1, blocking collectives  146 us
    dot_general x8, matrix products, one_term(): jnp.einsum('bpxz,pbzy->bpxy', mixed_half, gathered, preferred_element_typ...  83.7 us
    dot_general x8, matrix products, one_term(): jnp.einsum('pq,bqxz->bpxz', matrix, applied_left, preferred_element_type=...  43.4 us
    another operation x1, loops' own time, body(): lax.scan(one_term, jnp.zeros(two_site.shape, jnp.float32), (term_left, pi...  28.2 us
    dot_general x8, matrix products, one_term(): jnp.einsum('bxy,bqyz->bqxz', left_block, clean, preferred_element_type=jn...  28.2 us
    gather x8, local copies, waits for them, and re-layouts, one_term(): lax.dynamic_slice_in_dim(right_rows, begin, blocks, 0)  24.1 us
    dynamic_slice x16, local copies, waits for them, and re-layouts, body(): lax.scan(one_term, jnp.zeros(two_site.shape, jnp.float32), (term_left, pi...  9.5 us
  transfers between devices with their start and end apart: 2, of which 1 were waited for; matrix products, arithmetic and copies ran while one was open for 2% of the time, Pallas kernels for 0%

commit v1 on v0

v1 whole, which is shorter than its diff:
```python
import functools

import jax
import jax.numpy as jnp
from jax import lax
from jax.experimental import pallas as pl
from jax.experimental.pallas import tpu as pltpu
from jax.sharding import PartitionSpec as P

BF, F32, I32 = jnp.bfloat16, jnp.float32, jnp.int32
ROWS = 16
VMEM_LIMIT = 60 * 2**20


def dot(a, b):
    return jnp.dot(a, b, preferred_element_type=F32)


def iota(shape, axis):
    return lax.broadcasted_iota(I32, shape, axis)


def pack_kernel(left_ref, right_ref, terms_ref, packed_ref):
    terms, states, _ = terms_ref.shape
    packed_ref[...] = jnp.zeros_like(packed_ref)
    packed_ref[:, :, :states] = terms_ref[...]
    lane = iota((states, packed_ref.shape[2]), 1)
    for t in range(terms):
        row = packed_ref[t].astype(F32)
        row = jnp.where(lane == states, left_ref[t].astype(F32), row)
        row = jnp.where(lane == states + 1, right_ref[t].astype(F32), row)
        packed_ref[t] = row.astype(BF)


def gathered(mine, axis):
    count = lax.axis_size(axis)
    turns = [[(m, (m + turn) % count) for m in range(count)] for turn in range(1, count)]
    return jnp.stack([mine, *(lax.ppermute(mine, axis, pairs) for pairs in turns)])


def pack(term_left, term_right, mpo_terms):
    terms, states, _ = mpo_terms.shape
    smem = pl.BlockSpec(memory_space=pltpu.SMEM)
    vmem = pl.BlockSpec(memory_space=pltpu.VMEM)
    return pl.pallas_call(
        pack_kernel,
        out_shape=jax.ShapeDtypeStruct((terms, states, 128), BF),
        in_specs=[smem, smem, vmem],
        out_specs=vmem,
        name="pack_terms",
    )(term_left, term_right, mpo_terms)


def spread_terms(packed, spread, own, mine):
    terms, states, depth = packed.shape
    held, width = terms * own, states * ROWS
    row, col = iota((held, terms * states), 0), iota((held, terms * states), 1)
    pick = jnp.where(col == (row // own) * states + mine + row % own, 1.0, 0.0).astype(BF)
    wide = iota((depth, width), 0) == iota((depth, width), 1) // ROWS
    chosen = dot(pick, packed[...].reshape(terms * states, depth)).astype(BF)
    chosen = dot(chosen, jnp.where(wide, 1.0, 0.0).astype(BF))
    diagonal = iota((ROWS, width), 0) == iota((ROWS, width), 1) % ROWS
    for r in range(held):
        line = jnp.broadcast_to(chosen[r : r + 1, :], (ROWS, width))
        spread[r * ROWS : (r + 1) * ROWS, :] = jnp.where(diagonal, line, 0.0).astype(BF)


def block_kernel(edges, start, stop, own, total, *refs):
    refs = list(refs)
    shifts, sizes, packed = refs[:3]
    refs = refs[3:]
    first_call = start == 1 and not edges
    if not first_call:
        spread, _ = refs[:2]
        refs = refs[2:]
    two, left, right = refs[:3]
    refs = refs[3:]
    if edges:
        halo = refs[:4]
        refs = refs[4:]
    out = refs.pop(0)
    if first_call:
        spread = refs.pop(0)
    clean, lefts, rights, mixed, joined, result, wide, index, sems, out_sems = refs

    blocks, states, depth, _ = two.shape
    terms = packed.shape[0]
    bonds = left.shape[0]
    me = lax.axis_index("mpo")
    first = lax.axis_index("blk") * blocks
    mine = me * own

    if edges:
        count = 2
        half = halo[0].shape[0]
        core = lax.rem(me, 2)
        place = lambda n: n * (blocks - 1)
    else:
        count = stop - start
        place = lambda n: start + n

    def two_copy(n):
        return pltpu.make_async_copy(two.at[place(n)], clean.at[n], sems.at[0, n])

    def left_copy(n):
        return pltpu.make_async_copy(left.at[:, place(n)], lefts.at[n], sems.at[1, n])

    def right_copies(slot):
        if not edges:
            return [pltpu.make_async_copy(right.at[:, start - 1 + slot], rights.at[slot], sems.at[2, slot])]
        if slot in (0, 5):
            side = 0 if slot == 0 else 2
            return [
                pltpu.make_async_copy(
                    halo[side], rights.at[slot, pl.ds(core * half, half)], sems.at[2, slot]
                ),
                pltpu.make_async_copy(
                    halo[side + 1],
                    rights.at[slot, pl.ds((1 - core) * half, half)],
                    sems.at[2, slot + 1 if slot == 0 else slot + 2],
                ),
            ]
        block = slot - 1 if slot < 3 else blocks - 5 + slot
        return [pltpu.make_async_copy(right.at[:, block], rights.at[slot], sems.at[2, slot + 1])]

    def right_wait(slot):
        pltpu.make_async_copy(right.at[:, 0], rights.at[slot], sems.at[2, slot]).wait()

    two_copy(0).start()
    slots = 6 if edges else count + 2
    for n in range(count):
        news = ([0, 1, 2] if n == 0 else [3, 4, 5]) if edges else ([0, 1, 2] if n == 0 else [n + 2])
        for slot in news:
            for copy in right_copies(slot):
                copy.start()
        left_copy(n).start()
        if n + 1 < count:
            two_copy(n + 1).start()

    wide[...] = packed[:, 0, :].astype(F32).astype(I32)
    index_copy = pltpu.make_async_copy(wide, index, out_sems.at[count])
    index_copy.start()
    if first_call:
        spread_terms(packed, spread, own, mine)
    index_copy.wait()

    if edges:
        for slot in range(6):
            for copy in right_copies(slot):
                copy.wait()
    else:
        right_wait(0)
        right_wait(1)

    @pl.loop(0, count)
    def _(n):
        i = place(n)
        size = sizes[first + i]

        def width(p):
            j = first + i + shifts[p]
            return jnp.where((j >= 0) & (j < total), sizes[jnp.clip(j, 0, total - 1)], 0)

        two_copy(n).wait()
        keep_rows = jnp.where(iota((depth, depth), 0) < size, 1.0, 0.0).astype(BF)
        lane = iota((ROWS, depth), 1)
        for q in range(states):
            keep_cols = jnp.where(lane < width(q), 1.0, 0.0).astype(BF)
            block = clean[n, q].reshape(depth // ROWS, ROWS, depth) * keep_cols[None]
            clean[n, q] = block.reshape(depth, depth) * keep_rows

        for h in range(depth // (2 * ROWS)):
            spans = [slice((2 * h + u) * ROWS, (2 * h + u + 1) * ROWS) for u in range(2)]
            both = jnp.concatenate(
                [clean[n, :, s, :].reshape(states * ROWS, depth) for s in spans], axis=1
            )
            part = dot(spread[...], both).astype(BF).reshape(terms, own, ROWS, 2 * depth)
            for u in range(2):
                mixed[:, :, spans[u], :] = part[:, :, :, u * depth : (u + 1) * depth]

        if not edges:
            right_wait(n + 2)
        base = n * 3 + 1 if edges else n + 1
        slot_of = [base + shifts[mine + p] for p in range(own)]
        for t in range(terms):
            bond = index[t, states + 1]
            for p in range(own):
                joined[t, :, p * depth : (p + 1) * depth] = dot(
                    mixed[t, p], rights[slot_of[p], bond]
                ).astype(BF)

        left_copy(n).wait()
        row = jnp.concatenate([lefts[n, index[t, states]] for t in range(terms)], axis=1)
        summed = dot(row, joined[...].reshape(terms * depth, own * depth))
        rows, cols = iota((depth, depth), 0), iota((depth, depth), 1)
        for p in range(own):
            keep = (rows < size) & (cols < width(mine + p))
            result[n, p] = jnp.where(keep, summed[:, p * depth : (p + 1) * depth], 0.0).astype(BF)
        pltpu.make_async_copy(result.at[n], out.at[i], out_sems.at[n]).start()

    for n in range(count):
        pltpu.make_async_copy(result.at[n], out.at[place(n)], out_sems.at[n]).wait()


def apply_blocks(edges, start, stop, own, total, shifts, sizes, packed, carried, two, left, right, halo):
    blocks, states, depth, _ = two.shape
    terms, bonds = packed.shape[0], left.shape[0]
    count = 2 if edges else stop - start
    slots = 6 if edges else count + 2
    smem = pl.BlockSpec(memory_space=pltpu.SMEM)
    vmem = pl.BlockSpec(memory_space=pltpu.VMEM)
    anyw = pl.BlockSpec(memory_space=pl.ANY)
    out_shape = jax.ShapeDtypeStruct((blocks, own, depth, depth), BF)
    spread_shape = jax.ShapeDtypeStruct((terms * own * ROWS, states * ROWS), BF)
    operands = [shifts, sizes, packed]
    in_specs = [smem, smem, vmem]
    if carried is None:
        out_shapes, out_specs, aliases = (out_shape, spread_shape), (anyw, vmem), {}
    else:
        operands += [carried[1], carried[0]]
        in_specs += [vmem, anyw]
        out_shapes, out_specs, aliases = out_shape, anyw, {4: 0}
    operands += [two, left, right, *halo]
    in_specs += [anyw] * (3 + len(halo))
    flops = 2 * count * terms * own * depth**2 * (2 * depth + states * ROWS)
    moved = 2 * depth**2 * (count * (states + bonds + own) + slots * bonds)
    result = pl.pallas_call(
        functools.partial(block_kernel, edges, start, stop, own, total),
        out_shape=out_shapes,
        in_specs=in_specs,
        out_specs=out_specs,
        input_output_aliases=aliases,
        scratch_shapes=[
            pltpu.VMEM((count, states, depth, depth), BF),
            pltpu.VMEM((count, bonds, depth, depth), BF),
            pltpu.VMEM((slots, bonds, depth, depth), BF),
            pltpu.VMEM((terms, own, depth, depth), BF),
            pltpu.VMEM((terms, depth, own * depth), BF),
            pltpu.VMEM((count, own, depth, depth), BF),
            pltpu.VMEM((terms, 128), I32),
            pltpu.SMEM((terms, 128), I32),
            pltpu.SemaphoreType.DMA((3, slots + 2)),
            pltpu.SemaphoreType.DMA((count + 1,)),
        ],
        compiler_params=pltpu.CompilerParams(vmem_limit_bytes=VMEM_LIMIT),
        cost_estimate=pl.CostEstimate(flops=flops, bytes_accessed=moved, transcendentals=0),
        name="edge_blocks" if edges else "inner_blocks",
    )(*operands)
    return result if carried is None else (result, carried[1])


def body(two_site, left_env, right_env, mpo_terms, term_left, term_right, shifts, block_sizes):
    blocks, states = two_site.shape[:2]
    bonds = right_env.shape[0]
    groups, count = lax.axis_size("mpo"), lax.axis_size("blk")
    own, total = states // groups, blocks * count
    half = bonds // 2
    core = lax.rem(lax.axis_index("mpo"), 2)

    up = [(b, b + 1) for b in range(count - 1)]
    down = [(b + 1, b) for b in range(count - 1)]
    swap = [(m, m ^ 1) for m in range(groups)]
    edge = (half, 1, *right_env.shape[2:])
    tail = lax.dynamic_slice(right_env, (core * half, blocks - 1, 0, 0), edge).reshape(half, *edge[2:])
    head = lax.dynamic_slice(right_env, (core * half, 0, 0, 0), edge).reshape(half, *edge[2:])
    below = lax.ppermute(tail, "blk", up)
    above = lax.ppermute(head, "blk", down)

    packed = gathered(pack(term_left, term_right, mpo_terms), "mpo")
    packed = packed.reshape(-1, *packed.shape[2:])
    arrays = (two_site, left_env, right_env)
    sides = (own, total, shifts, block_sizes, packed)
    done = apply_blocks(False, 1, blocks - 1, *sides, None, *arrays, ())
    below, above, done = lax.optimization_barrier((below, above, done))
    below_too = lax.ppermute(below, "mpo", swap)
    above_too = lax.ppermute(above, "mpo", swap)
    done = apply_blocks(True, 0, 0, *sides, done, *arrays, (below, below_too, above, above_too))
    return done[0]


def solution(mesh):
    return jax.shard_map(
        body,
        mesh=mesh,
        in_specs=(
            P("blk", None, None, None),
            P(None, "blk", None, None),
            P(None, "blk", None, None),
            P("mpo", None, None),
            P("mpo"),
            P("mpo"),
            P(),
            P(),
        ),
        out_specs=P("blk", "mpo", None, None),
        check_vma=False,
    )
```

time: 411 us -> 54.4 us (0.13)
  matrix products: 155 us -> 0 us
  blocking collectives: 146 us -> 0 us
  local copies, waits for them, and re-layouts: 50.3 us -> 2.19 us
  Pallas kernels: 0 us -> 38.1 us
  loops' own time: 28.2 us -> 0 us
  other arithmetic: 17.3 us -> 1.43 us
    dot_general x24 -> x0, matrix products: 155 us -> none  [the longest x8 83.7 us: one_term(): jnp.einsum('bpxz,pbzy->bpxy', mixed_half, gathered, preferred_element_typ...]
    unnamed x1 -> x0, blocking collectives: 146 us -> none
    pallas_call x0 -> x3, Pallas kernels: none -> 38.1 us  [the longest x2 36.6 us: apply_blocks(): pl.pallas_call(functools.partial(block_kernel, edges, start, stop, own, t...]
    gather x9 -> x0, local copies, waits for them, and re-layouts: 29.8 us -> none  [the longest x8 24.1 us: one_term(): lax.dynamic_slice_in_dim(right_rows, begin, blocks, 0)]
    another operation x1 -> x0, loops' own time: 28.2 us -> none  [body(): lax.scan(one_term, jnp.zeros(two_site.shape, jnp.float32), (term_left, pi...]
    select_n x4 -> x0, other arithmetic: 14 us -> none  [the longest x1 6.44 us: body(): masked = jnp.where(mask, summed, jnp.float32(0.0))]
    dynamic_slice x16 -> x0, local copies, waits for them, and re-layouts: 9.5 us -> none  [body(): lax.scan(one_term, jnp.zeros(two_site.shape, jnp.float32), (term_left, pi...]
    squeeze x8 -> x0, local copies, waits for them, and re-layouts: 8 us -> none  [one_term(): lax.dynamic_index_in_dim(padded, right_index, 0, keepdims=False)]
  transfers between devices with their start and end apart: 2 -> 7, of which waited for: 1 -> 2; matrix products, arithmetic and copies ran while one was open for 2% -> 5% of each run, Pallas kernels for 0% -> 45%
where the time goes in v1:
time: 54.4 us; the launch traced here: 54.1 us
  Pallas kernels  38.1 us (70%)
  starting transfers between devices  10 us (18%)
  waiting for transfers between devices  2.31 us (4%)
  local copies, waits for them, and re-layouts  2.19 us (4%)
  other arithmetic  1.43 us (3%)
    pallas_call x2, Pallas kernels, apply_blocks(): pl.pallas_call(functools.partial(block_kernel, edges, start, stop, own, t...  36.6 us
    ppermute x1, starting transfers between devices, body(): below = lax.ppermute(tail, 'blk', up)  4.58 us
    ppermute x3, starting transfers between devices, gathered(): lax.ppermute(mine, axis, pairs)  3.2 us
    ppermute x1, waiting for transfers between devices, body(): below_too = lax.ppermute(below, 'mpo', swap)  1.5 us
    another operation x1, other arithmetic, gathered(): jnp.stack([mine, *(lax.ppermute(mine, axis, pairs) for pairs in turns)])  1.43 us
    pallas_call x1, Pallas kernels, pack(): pl.pallas_call(pack_kernel, out_shape=jax.ShapeDtypeStruct((terms, states...  1.41 us
    reshape x1, local copies, waits for them, and re-layouts, body(): lax.dynamic_slice(right_env, (core * half, 0, 0, 0), edge)  1.34 us
    ppermute x1, starting transfers between devices, body(): above = lax.ppermute(head, 'blk', down)  1.29 us
  transfers between devices with their start and end apart: 7, of which 2 were waited for; matrix products, arithmetic and copies ran while one was open for 5% of the time, Pallas kernels for 45%

profile of v1, /device:TPU:0, one launch (start us, length us, event | category | flops | bytes accessed | tf_op | source)
XLA Modules:
  0.0 54.1 jit_solution(7099456962685664942)
XLA Ops:
  0.0 1.4 %pack_terms.1 = bf16[8,16,128]{2,1,0:T(8,128)(2,1)} custom-call(s32[8]{0:T(128)} %left_ref.1, s32[8]{0:T(128)} %right_ref.1, bf16[8,16,16]{2,1,0:T(8,128)(2,1)} %terms_ref.1), custom_call_target="tpu_custom_call" | custom-call | tf_op jit(solution)/shard_map/pack_terms/pallas_call | solution.py:45
  1.4 2.4 %collective-permute-start.2 = (bf16[8,16,128]{2,1,0:T(8,128)(2,1)}, bf16[8,16,128]{2,1,0:T(8,128)(2,1)S(1)}, u32[]{:S(2)}, u32[]{:S(2)}) collective-permute-start(bf16[8,16,128]{2,1,0:T(8,128)(2,1)} %pack_terms.1), channel_id=1, source_target_pairs={{0,24},{8,0},{16,8},{24,16},{1,25},{9,1},{17,9},{25,17},{2,26},{10... | collective-permute-start | bytes 98312 | tf_op jit(solution)/shard_map/ppermute | solution.py:38
  3.8 0.6 %collective-permute-start.1 = (bf16[8,16,128]{2,1,0:T(8,128)(2,1)}, bf16[8,16,128]{2,1,0:T(8,128)(2,1)S(1)}, u32[]{:S(2)}, u32[]{:S(2)}) collective-permute-start(bf16[8,16,128]{2,1,0:T(8,128)(2,1)} %pack_terms.1), channel_id=1, source_target_pairs={{0,16},{8,24},{16,0},{24,8},{1,17},{9,25},{17,1},{25,9},{2,18},{10... | collective-permute-start | bytes 98312 | tf_op jit(solution)/shard_map/ppermute | solution.py:38
  4.4 0.2 collective-permute-start
  4.6 1.3 %dynamic-slice_bitcast_fusion = (bf16[17,128,128]{2,1,0:T(8,128)(2,1)S(1)}, bf16[17,128,128]{2,1,0:T(8,128)(2,1)S(1)}) fusion(bf16[34,8,128,128]{3,2,1,0:T(8,128)(2,1)} %refs_7_.1, s32[]{:T(128)S(6)} %select_n.4), kind=kLoop, calls=%fused_computation | loop fusion | bytes 2228228 | tf_op jit(solution)/shard_map/reshape | solution.py:265
  6.0 1.3 %collective-permute-start.4 = (bf16[17,128,128]{2,1,0:T(8,128)(2,1)S(1)}, bf16[17,128,128]{2,1,0:T(8,128)(2,1)S(1)}, u32[]{:S(2)}, u32[]{:S(2)}) collective-permute-start(bf16[17,128,128]{2,1,0:T(8,128)(2,1)S(1)} %get-tuple-element.17), channel_id=1, source_target_pairs={{1,0},{2,1},{3,2},{4,3},{5,4},{6,5},{7,6},{9,8},{10,9},{11,10},{12... | collective-permute-start | bytes 1671176 | tf_op jit(solution)/shard_map/ppermute | solution.py:267
  7.3 4.6 %collective-permute-start.3 = (bf16[17,128,128]{2,1,0:T(8,128)(2,1)S(1)}, bf16[17,128,128]{2,1,0:T(8,128)(2,1)S(1)}, u32[]{:S(2)}, u32[]{:S(2)}) collective-permute-start(bf16[17,128,128]{2,1,0:T(8,128)(2,1)S(1)} %get-tuple-element.18), channel_id=1, source_target_pairs={{0,1},{1,2},{2,3},{3,4},{4,5},{5,6},{6,7},{8,9},{9,10},{10,11},{11... | collective-permute-start | bytes 1671176 | tf_op jit(solution)/shard_map/ppermute | solution.py:266
  11.8 0.0 collective-permute-done.2
  11.9 0.0 collective-permute-done.1
  11.9 0.0 collective-permute-done
  11.9 1.4 %pad_maximum_fusion = bf16[4,8,16,128]{3,2,1,0:T(8,128)(2,1)} fusion(bf16[1,8,16,128]{3,2,1,0:T(8,128)(2,1)S(1)} %bitcast.12, bf16[1,8,16,128]{3,2,1,0:T(8,128)(2,1)S(1)} %bitcast.13, bf16[1,8,16,128]{3,2,1,0:T(8,128)(2,1)S(1)} %bitcast.14, bf16[1,8,16,128]{3,2,1,0:T(8,128)(2,1)} %bitcast.11), kind=kLoop, calls=%fused_computation.2 | loop fusion | flops 196608 | bytes 262144 | tf_op jit(solution)/shard_map/stack | solution.py:38
  13.3 24.5 %inner_blocks.1 = (bf16[8,4,128,128]{3,2,1,0:T(8,128)(2,1)}, bf16[2048,256]{1,0:T(8,128)(2,1)}) custom-call(s32[16]{0:T(128)} %refs_0_.3, s32[64]{0:T(128)} %refs_1_.3, bf16[32,16,128]{2,1,0:T(8,128)(2,1)} %bitcast.9, bf16[8,16,128,128]{3,2,1,0:T(8,128)(2,1)} %refs_5_.3, bf16[34,8,128,128]{3,2,1,0:T(8,128)(2,1)} %refs_6_.1, bf16[34,8,128,128]{3,2,1,0:T(8,128)(2,1)} %refs_7_.1), custom_call_target="tpu_custom_call" | custom-call | flops 12884901888 | bytes 19529728 | tf_op jit(solution)/shard_map/inner_blocks/pallas_call | solution.py:227
  37.8 0.0 collective-permute-done.4.refs_10_
  37.8 0.0 copy-start
  37.9 0.0 collective-permute-done.3.refs_8_
  37.9 0.0 copy-start.1
  37.9 0.9 %collective-permute-start.5 = (bf16[17,128,128]{2,1,0:T(8,128)(2,1)S(1)}, bf16[17,128,128]{2,1,0:T(8,128)(2,1)S(1)}, u32[]{:S(2)}, u32[]{:S(2)}) collective-permute-start(bf16[17,128,128]{2,1,0:T(8,128)(2,1)S(1)} %collective-permute-done.3.refs_8_), channel_id=1, source_target_pairs={{0,8},{8,0},{16,24},{24,16},{1,9},{9,1},{17,25},{25,17},{2,10},{10... | collective-permute-start | bytes 1671176 | tf_op jit(solution)/shard_map/ppermute | solution.py:275
  38.7 0.1 collective-permute-start.6
  38.8 1.5 %collective-permute-done.5.refs_9_ = bf16[17,128,128]{2,1,0:T(8,128)(2,1)S(1)} collective-permute-done((bf16[17,128,128]{2,1,0:T(8,128)(2,1)S(1)}, bf16[17,128,128]{2,1,0:T(8,128)(2,1)S(1)}, u32[]{:S(2)}, u32[]{:S(2)}) %collective-permute-start.5) | collective-permute-done | bytes 557088 | tf_op jit(solution)/shard_map/ppermute | solution.py:275
  40.3 0.8 %collective-permute-done.6.refs_11_ = bf16[17,128,128]{2,1,0:T(8,128)(2,1)S(1)} collective-permute-done((bf16[17,128,128]{2,1,0:T(8,128)(2,1)S(1)}, bf16[17,128,128]{2,1,0:T(8,128)(2,1)S(1)}, u32[]{:S(2)}, u32[]{:S(2)}) %collective-permute-start.6) | collective-permute-done | bytes 557088 | tf_op jit(solution)/shard_map/ppermute | solution.py:276
  41.1 0.0 copy-done
  41.1 0.0 copy-done.2
  41.2 0.8 %copy-done.3 = bf16[17,128,128]{2,1,0:T(8,128)(2,1)} copy-done((bf16[17,128,128]{2,1,0:T(8,128)(2,1)}, bf16[17,128,128]{2,1,0:T(8,128)(2,1)S(1)}, u32[]{:S(2)}) %copy-start.3) | copy-done | bytes 557080
  42.0 12.1 %edge_blocks.1 = bf16[8,4,128,128]{3,2,1,0:T(8,128)(2,1)} custom-call(s32[16]{0:T(128)} %refs_0_.3, s32[64]{0:T(128)} %refs_1_.3, bf16[32,16,128]{2,1,0:T(8,128)(2,1)} %bitcast.10, bf16[2048,256]{1,0:T(8,128)(2,1)} %get-tuple-element.13.refs_3_, bf16[8,4,128,128]{3,2,1,0:T(8,128)(2,1)} %get-tuple-element.14.refs_4_, ...), custom_call_target="tpu_custom_call", output_to_operand_aliasing={{}: (4, {})} | custom-call | flops 4294967296 | bytes 10223616 | tf_op jit(solution)/shard_map/edge_blocks/pallas_call | solution.py:227
  (3 shorter events, 0.0 us)
Async XLA Ops:
  1.4 10.4 %collective-permute-start.2 = (bf16[8,16,128]{2,1,0:T(8,128)(2,1)}, bf16[8,16,128]{2,1,0:T(8,128)(2,1)S(1)}, u32[]{:S(2)}, u32[]{:S(2)}) collective-permute-start(bf16[8,16,128]{2,1,0:T(8,128)(2,1)} %pack_terms.1), channel_id=1, source_target_pairs={{0,24},{8,0},{16,8},{24,16},{1,25},{9,1},{17,9},{25,17},{2,26},{10... | collective-permute-start | bytes 98312 | tf_op jit(solution)/shard_map/ppermute | solution.py:38
  3.8 8.0 %collective-permute-start.1 = (bf16[8,16,128]{2,1,0:T(8,128)(2,1)}, bf16[8,16,128]{2,1,0:T(8,128)(2,1)S(1)}, u32[]{:S(2)}, u32[]{:S(2)}) collective-permute-start(bf16[8,16,128]{2,1,0:T(8,128)(2,1)} %pack_terms.1), channel_id=1, source_target_pairs={{0,16},{8,24},{16,0},{24,8},{1,17},{9,25},{17,1},{25,9},{2,18},{10... | collective-permute-start | bytes 98312 | tf_op jit(solution)/shard_map/ppermute | solution.py:38
  4.4 7.5 %collective-permute-start = (bf16[8,16,128]{2,1,0:T(8,128)(2,1)}, bf16[8,16,128]{2,1,0:T(8,128)(2,1)S(1)}, u32[]{:S(2)}, u32[]{:S(2)}) collective-permute-start(bf16[8,16,128]{2,1,0:T(8,128)(2,1)} %pack_terms.1), channel_id=1, source_target_pairs={{0,8},{8,16},{16,24},{24,0},{1,9},{9,17},{17,25},{25,1},{2,10},{10... | collective-permute-start | bytes 98312 | tf_op jit(solution)/shard_map/ppermute | solution.py:38
  6.0 31.9 %collective-permute-start.4 = (bf16[17,128,128]{2,1,0:T(8,128)(2,1)S(1)}, bf16[17,128,128]{2,1,0:T(8,128)(2,1)S(1)}, u32[]{:S(2)}, u32[]{:S(2)}) collective-permute-start(bf16[17,128,128]{2,1,0:T(8,128)(2,1)S(1)} %get-tuple-element.17), channel_id=1, source_target_pairs={{1,0},{2,1},{3,2},{4,3},{5,4},{6,5},{7,6},{9,8},{10,9},{11,10},{12... | collective-permute-start | bytes 1671176 | tf_op jit(solution)/shard_map/ppermute | solution.py:267
  7.3 30.6 %collective-permute-start.3 = (bf16[17,128,128]{2,1,0:T(8,128)(2,1)S(1)}, bf16[17,128,128]{2,1,0:T(8,128)(2,1)S(1)}, u32[]{:S(2)}, u32[]{:S(2)}) collective-permute-start(bf16[17,128,128]{2,1,0:T(8,128)(2,1)S(1)} %get-tuple-element.18), channel_id=1, source_target_pairs={{0,1},{1,2},{2,3},{3,4},{4,5},{5,6},{6,7},{8,9},{9,10},{10,11},{11... | collective-permute-start | bytes 1671176 | tf_op jit(solution)/shard_map/ppermute | solution.py:266
  37.8 3.3 %copy-start = (bf16[17,128,128]{2,1,0:T(8,128)(2,1)}, bf16[17,128,128]{2,1,0:T(8,128)(2,1)S(1)}, u32[]{:S(2)}) copy-start(bf16[17,128,128]{2,1,0:T(8,128)(2,1)S(1)} %collective-permute-done.4.refs_10_) | copy-start | bytes 1671172
  37.9 3.2 %copy-start.1 = (bf16[17,128,128]{2,1,0:T(8,128)(2,1)}, bf16[17,128,128]{2,1,0:T(8,128)(2,1)S(1)}, u32[]{:S(2)}) copy-start(bf16[17,128,128]{2,1,0:T(8,128)(2,1)S(1)} %collective-permute-done.3.refs_8_) | copy-start | bytes 1671172
  37.9 2.4 %collective-permute-start.5 = (bf16[17,128,128]{2,1,0:T(8,128)(2,1)S(1)}, bf16[17,128,128]{2,1,0:T(8,128)(2,1)S(1)}, u32[]{:S(2)}, u32[]{:S(2)}) collective-permute-start(bf16[17,128,128]{2,1,0:T(8,128)(2,1)S(1)} %collective-permute-done.3.refs_8_), channel_id=1, source_target_pairs={{0,8},{8,0},{16,24},{24,16},{1,9},{9,1},{17,25},{25,17},{2,10},{10... | collective-permute-start | bytes 1671176 | tf_op jit(solution)/shard_map/ppermute | solution.py:275
  38.7 2.4 %collective-permute-start.6 = (bf16[17,128,128]{2,1,0:T(8,128)(2,1)S(1)}, bf16[17,128,128]{2,1,0:T(8,128)(2,1)S(1)}, u32[]{:S(2)}, u32[]{:S(2)}) collective-permute-start(bf16[17,128,128]{2,1,0:T(8,128)(2,1)S(1)} %collective-permute-done.4.refs_10_), channel_id=1, source_target_pairs={{0,8},{8,0},{16,24},{24,16},{1,9},{9,1},{17,25},{25,17},{2,10},{10... | collective-permute-start | bytes 1671176 | tf_op jit(solution)/shard_map/ppermute | solution.py:276
  40.3 0.8 %copy-start.2 = (bf16[17,128,128]{2,1,0:T(8,128)(2,1)}, bf16[17,128,128]{2,1,0:T(8,128)(2,1)S(1)}, u32[]{:S(2)}) copy-start(bf16[17,128,128]{2,1,0:T(8,128)(2,1)S(1)} %collective-permute-done.5.refs_9_) | copy-start | bytes 1671172
  41.2 0.8 %copy-start.3 = (bf16[17,128,128]{2,1,0:T(8,128)(2,1)}, bf16[17,128,128]{2,1,0:T(8,128)(2,1)S(1)}, u32[]{:S(2)}) copy-start(bf16[17,128,128]{2,1,0:T(8,128)(2,1)S(1)} %collective-permute-done.6.refs_11_) | copy-start | bytes 1671172

commit v2 on v0

v2 whole, which is shorter than its diff:
```python
import functools
import math

import jax
import jax.numpy as jnp
from jax import lax
from jax.experimental import pallas as pl
from jax.experimental.pallas import tpu as pltpu
from jax.sharding import PartitionSpec as P

BF, F32, I32 = jnp.bfloat16, jnp.float32, jnp.int32
ROWS = 16
LANES = 128
SPARE_VMEM = 12 * 2**20
MOST_VMEM = 60 * 2**20


def dot(a, b):
    return jnp.dot(a, b, preferred_element_type=F32)


def iota(shape, axis):
    return lax.broadcasted_iota(I32, shape, axis)


def gathered(mine, axis):
    count = lax.axis_size(axis)
    turns = [[(m, (m + turn) % count) for m in range(count)] for turn in range(1, count)]
    return [mine, *(lax.ppermute(mine, axis, pairs) for pairs in turns)]


def ready_kernel(left_ref, right_ref, terms_ref, env_ref, packed_ref, sent_ref, sem):
    terms, states, _ = terms_ref.shape
    core = lax.rem(lax.axis_index("mpo"), 2)
    edge = (1 - core) * (env_ref.shape[1] - 1)
    copy = pltpu.make_async_copy(env_ref.at[:, edge], sent_ref, sem)
    copy.start()
    packed_ref[...] = jnp.zeros_like(packed_ref)
    packed_ref[:, :, :states] = terms_ref[...]
    lane = iota((states, LANES), 1)
    for t in range(terms):
        row = packed_ref[t].astype(F32)
        row = jnp.where(lane == states, left_ref[t].astype(F32), row)
        row = jnp.where(lane == states + 1, right_ref[t].astype(F32), row)
        packed_ref[t] = row.astype(BF)
    copy.wait()


def ready(term_left, term_right, mpo_terms, right_env):
    terms, states, _ = mpo_terms.shape
    bonds, _, depth, _ = right_env.shape
    smem = pl.BlockSpec(memory_space=pltpu.SMEM)
    vmem = pl.BlockSpec(memory_space=pltpu.VMEM)
    anyw = pl.BlockSpec(memory_space=pl.ANY)
    return pl.pallas_call(
        ready_kernel,
        out_shape=[
            pltpu.VMEM((terms, states, LANES), BF),
            pltpu.VMEM((bonds, depth, depth), BF),
        ],
        in_specs=[smem, smem, vmem, anyw],
        out_specs=[vmem, vmem],
        scratch_shapes=[pltpu.SemaphoreType.DMA],
        name="ready",
    )(term_left, term_right, mpo_terms, right_env)


def spread_terms(packed, spread, own, mine):
    terms, states, _ = packed.shape
    width, rows = states * ROWS, own * ROWS
    pick = jnp.where(iota((rows, states), 1) == mine + iota((rows, states), 0) // ROWS, 1.0, 0.0).astype(BF)
    widen = jnp.where(iota((LANES, width), 0) == iota((LANES, width), 1) // ROWS, 1.0, 0.0).astype(BF)
    diagonal = jnp.where(iota((ROWS, width), 0) == iota((ROWS, width), 1) % ROWS, 1.0, 0.0).astype(BF)
    wide = dot(packed[...].reshape(terms * states, LANES), widen).astype(BF)
    for t in range(terms):
        chosen = dot(pick, wide[t * states : (t + 1) * states, :]).astype(BF)
        chosen = chosen.reshape(own, ROWS, width) * diagonal[None]
        spread[t * rows : (t + 1) * rows, :] = chosen.reshape(rows, width)


def block_kernel(edge, count, own, total, *refs):
    refs = list(refs)
    pieces = [refs.pop(0) for _ in range(lax.axis_size("mpo"))]
    numbers = [refs.pop(0) for _ in range(2)]
    if edge:
        refs.pop(0)
        halo = refs.pop(0)
    two, left, right, out = (refs.pop(0) for _ in range(4))
    if edge:
        passed = refs.pop(0)
    packed, spread, clean, lefts, rights, mixed, joined, result, wide, index, shifts, sizes, sems = refs

    blocks, states, depth, _ = two.shape
    terms = packed.shape[0]
    share = terms // len(pieces)
    me = lax.axis_index("mpo")
    core = lax.rem(me, 2)
    first = lax.axis_index("blk") * blocks
    mine = (me - core) * (own // 2) if edge else me * own

    def place(n):
        return core * (blocks - 1) if edge else 1 + n

    def two_copy(n):
        return pltpu.make_async_copy(two.at[place(n)], clean.at[n], sems.at[0, n])

    def left_copy(n):
        return pltpu.make_async_copy(left.at[:, place(n)], lefts.at[n], sems.at[1, n])

    def right_copy(slot):
        if not edge:
            return pltpu.make_async_copy(right.at[:, slot], rights.at[slot], sems.at[2, slot])
        if slot == 0:
            return pltpu.make_async_copy(halo, rights.at[2 * core], sems.at[2, slot])
        near = place(0) + (0 if slot == 1 else 1 - 2 * core)
        return pltpu.make_async_copy(right.at[:, near], rights.at[1 if slot == 1 else 2 - 2 * core], sems.at[2, slot])

    def index_copy():
        return pltpu.make_async_copy(wide, index, sems.at[3, 0])

    small = [
        pltpu.make_async_copy(piece, packed.at[pl.ds(n * share, share)], sems.at[5, n])
        for n, piece in enumerate(pieces)
    ] + [pltpu.make_async_copy(a, b, sems.at[6, n]) for n, (a, b) in enumerate(zip(numbers, (shifts, sizes)))]
    for copy in small:
        copy.start()
    two_copy(0).start()

    def live(n, p=None):
        j = first + place(n) + (0 if p is None else shifts[p])
        return jnp.where((j >= 0) & (j < total), sizes[jnp.clip(j, 0, total - 1)], 0)

    def wipe(n):
        keep_rows = jnp.where(iota((depth, depth), 0) < live(n), 1.0, 0.0).astype(BF)
        lane = iota((ROWS, depth), 1)
        for q in range(states):
            keep_cols = jnp.where(lane < live(n, q), 1.0, 0.0).astype(BF)
            block = clean[n, q].reshape(depth // ROWS, ROWS, depth) * keep_cols[None]
            clean[n, q] = block.reshape(depth, depth) * keep_rows

    for copy in small:
        copy.wait()
    wide[...] = packed[:, 0, :].astype(F32).astype(I32)
    index_copy().start()
    spread_terms(packed, spread, own, mine)
    two_copy(0).wait()
    wipe(0)
    for n in range(count):
        for slot in (0, 1, 2) if n == 0 else (n + 2,):
            right_copy(slot).start()
        left_copy(n).start()
        if n + 1 < count:
            two_copy(n + 1).start()
    index_copy().wait()

    def apply(n):
        i = place(n)

        for h in range(depth // (2 * ROWS)):
            spans = [slice((2 * h + u) * ROWS, (2 * h + u + 1) * ROWS) for u in range(2)]
            both = jnp.concatenate(
                [clean[n, :, s, :].reshape(states * ROWS, depth) for s in spans], axis=1
            )
            part = dot(spread[...], both).astype(BF).reshape(terms, own, ROWS, 2 * depth)
            for u in range(2):
                mixed[:, :, spans[u], :] = part[:, :, :, u * depth : (u + 1) * depth]

        if edge:
            for slot in range(3):
                right_copy(slot).wait()
        else:

            @pl.when(n == 0)
            def _():
                right_copy(0).wait()
                right_copy(1).wait()

            right_copy(n + 2).wait()
        if not edge:
            later = jnp.minimum(n + 1, count - 1)

            @pl.when(n + 1 < count)
            def _():
                two_copy(n + 1).wait()

            wipe(later)
        slot_of = [(1 if edge else n + 1) + shifts[mine + p] for p in range(own)]
        for t in range(terms):
            bond = index[t, states + 1]
            for p in range(own):
                joined[t, :, p * depth : (p + 1) * depth] = dot(
                    mixed[t, p], rights[slot_of[p], bond]
                ).astype(BF)

        left_copy(n).wait()
        row = jnp.concatenate([lefts[n, index[t, states]] for t in range(terms)], axis=1)
        summed = dot(row, joined[...].reshape(terms * depth, own * depth))
        rows, cols = iota((depth, depth), 0), iota((depth, depth), 1)
        for p in range(own):
            keep = (rows < live(n)) & (cols < live(n, mine + p))
            result[n, p] = jnp.where(keep, summed[:, p * depth : (p + 1) * depth], 0.0).astype(BF)

    if edge:
        apply(0)
        half = own // 2
        ours = pltpu.make_async_copy(
            result.at[0, pl.ds(core * half, half)], out.at[place(0)], sems.at[0, 0]
        )
        theirs = pltpu.make_async_copy(
            result.at[0, pl.ds((1 - core) * half, half)], passed, sems.at[1, 0]
        )
        theirs.start()
        ours.start()
        theirs.wait()
        ours.wait()
    else:

        def out_copy(n):
            return pltpu.make_async_copy(result.at[n], out.at[place(n)], sems.at[4, n])

        @pl.loop(0, count)
        def _(n):
            apply(n)
            out_copy(n).start()

        for n in range(count):
            out_copy(n).wait()


def apply_blocks(edge, pieces, shifts, sizes, two, left, right, own, total, done=None, halo=None):
    blocks, states, depth, _ = two.shape
    terms, bonds = sum(piece.shape[0] for piece in pieces), left.shape[0]
    count = 1 if edge else blocks - 2
    slots = count + 2
    anyw = pl.BlockSpec(memory_space=pl.ANY)
    near = functools.partial(pltpu.with_memory_space_constraint, memory_space=pltpu.VMEM)
    far = functools.partial(pltpu.with_memory_space_constraint, memory_space=pltpu.HBM)
    operands = [*map(near, pieces), far(shifts), far(sizes)]
    operands += [far(done), near(halo)] if edge else []
    operands += map(far, (two, left, right))
    kept = own // 2 if edge else own
    out_shapes = [jax.ShapeDtypeStruct((blocks, kept, depth, depth), BF)]
    if edge:
        out_shapes.append(jax.ShapeDtypeStruct((kept, depth, depth), BF))
    buffers = [
        (terms, states, LANES),
        (terms * own * ROWS, states * ROWS),
        (count, states, depth, depth),
        (count, bonds, depth, depth),
        (slots, bonds, depth, depth),
        (terms, own, depth, depth),
        (terms, depth, own * depth),
        (count, own, depth, depth),
    ]
    held = sum(2 * math.prod(shape) for shape in buffers)
    flops = 2 * count * terms * own * depth**2 * (2 * depth + states * ROWS)
    moved = 2 * depth**2 * (count * (states + bonds + own) + slots * bonds)
    return pl.pallas_call(
        functools.partial(block_kernel, edge, count, own, total),
        out_shape=out_shapes,
        in_specs=[anyw] * len(operands),
        out_specs=[anyw] * len(out_shapes),
        input_output_aliases={len(pieces) + 2: 0} if edge else {},
        scratch_shapes=[
            *(pltpu.VMEM(shape, BF) for shape in buffers),
            pltpu.VMEM((terms, LANES), I32),
            pltpu.SMEM((terms, LANES), I32),
            pltpu.SMEM(shifts.shape, I32),
            pltpu.SMEM(sizes.shape, I32),
            pltpu.SemaphoreType.DMA((7, max(slots, len(pieces)))),
        ],
        compiler_params=pltpu.CompilerParams(vmem_limit_bytes=min(held + SPARE_VMEM, MOST_VMEM)),
        cost_estimate=pl.CostEstimate(flops=flops, bytes_accessed=moved, transcendentals=0),
        name="edge_block" if edge else "inner_blocks",
    )(*operands)


def body(two_site, left_env, right_env, mpo_terms, term_left, term_right, shifts, block_sizes):
    blocks, states = two_site.shape[:2]
    groups, count = lax.axis_size("mpo"), lax.axis_size("blk")
    own, total = states // groups, blocks * count
    core = lax.rem(lax.axis_index("mpo"), 2)

    packed, sent = ready(term_left, term_right, mpo_terms, right_env)
    pieces = gathered(packed, "mpo")

    place = lambda m, b: m * count + b
    up = [(place(m, b), place(m, b + 1)) for m in range(0, groups, 2) for b in range(count - 1)]
    down = [(place(m, b + 1), place(m, b)) for m in range(1, groups, 2) for b in range(count - 1)]
    halo = lax.ppermute(sent, ("mpo", "blk"), up + down)

    arrays = (pieces, shifts, block_sizes, two_site, left_env, right_env)
    (done,) = apply_blocks(False, *arrays, own, total)
    done, passed = apply_blocks(True, *arrays, 2 * own, total, done, halo)
    passed = lax.ppermute(passed, "mpo", [(m, m ^ 1) for m in range(groups)])
    return lax.dynamic_update_slice(done, passed[None], ((1 - core) * (blocks - 1), 0, 0, 0))


def solution(mesh):
    return jax.shard_map(
        body,
        mesh=mesh,
        in_specs=(
            P("blk", None, None, None),
            P(None, "blk", None, None),
            P(None, "blk", None, None),
            P("mpo", None, None),
            P("mpo"),
            P("mpo"),
            P(),
            P(),
        ),
        out_specs=P("blk", "mpo", None, None),
        check_vma=False,
    )
```

time: 411 us -> 45.8 us (0.11)
  matrix products: 155 us -> 0 us
  blocking collectives: 146 us -> 0 us
  local copies, waits for them, and re-layouts: 50.3 us -> 0.67 us
  Pallas kernels: 0 us -> 35.2 us
  loops' own time: 28.2 us -> 0 us
  other arithmetic: 17.3 us -> 0 us
    dot_general x24 -> x0, matrix products: 155 us -> none  [the longest x8 83.7 us: one_term(): jnp.einsum('bpxz,pbzy->bpxy', mixed_half, gathered, preferred_element_typ...]
    unnamed x1 -> x0, blocking collectives: 146 us -> none
    pallas_call x0 -> x3, Pallas kernels: none -> 35.2 us  [the longest x2 33.2 us: apply_blocks(): pl.pallas_call(functools.partial(block_kernel, edge, count, own, total),...]
    gather x9 -> x0, local copies, waits for them, and re-layouts: 29.8 us -> none  [the longest x8 24.1 us: one_term(): lax.dynamic_slice_in_dim(right_rows, begin, blocks, 0)]
    another operation x1 -> x0, loops' own time: 28.2 us -> none  [body(): lax.scan(one_term, jnp.zeros(two_site.shape, jnp.float32), (term_left, pi...]
    select_n x4 -> x0, other arithmetic: 14 us -> none  [the longest x1 6.44 us: body(): masked = jnp.where(mask, summed, jnp.float32(0.0))]
    dynamic_slice x16 -> x0, local copies, waits for them, and re-layouts: 9.5 us -> none  [body(): lax.scan(one_term, jnp.zeros(two_site.shape, jnp.float32), (term_left, pi...]
    squeeze x8 -> x0, local copies, waits for them, and re-layouts: 8 us -> none  [one_term(): lax.dynamic_index_in_dim(padded, right_index, 0, keepdims=False)]
  transfers between devices with their start and end apart: 2 -> 5, of which waited for: 1 -> 2; matrix products, arithmetic and copies ran while one was open for 2% -> 0% of each run, Pallas kernels for 0% -> 52%
where the time goes in v2:
time: 45.8 us; the launch traced here: 45.5 us
  Pallas kernels  35.2 us (77%)
  starting transfers between devices  8.01 us (17%)
  waiting for transfers between devices  1.54 us (3%)
  local copies, waits for them, and re-layouts  0.67 us (1%)
    pallas_call x2, Pallas kernels, apply_blocks(): pl.pallas_call(functools.partial(block_kernel, edge, count, own, total),...  33.2 us
    ppermute x3, starting transfers between devices, gathered(): return [mine, *(lax.ppermute(mine, axis, pairs) for pairs in turns)]  4.48 us
    ppermute x1, starting transfers between devices, body(): halo = lax.ppermute(sent, ('mpo', 'blk'), up + down)  3.45 us
    pallas_call x1, Pallas kernels, ready(): pl.pallas_call(ready_kernel, out_shape=[pltpu.VMEM((terms, states, LANES)...  2.05 us
    ppermute x1, waiting for transfers between devices, body(): passed = lax.ppermute(passed, 'mpo', [(m, m ^ 1) for m in range(groups)])  1.33 us
  transfers between devices with their start and end apart: 5, of which 2 were waited for; matrix products, arithmetic and copies ran while one was open for 0% of the time, Pallas kernels for 52%

profile of v2, /device:TPU:0, one launch (start us, length us, event | category | flops | bytes accessed | tf_op | source)
XLA Modules:
  0.0 45.5 jit_solution(2856365771512832422)
XLA Ops:
  0.0 2.0 %ready.1 = (bf16[8,16,128]{2,1,0:T(8,128)(2,1)S(1)}, bf16[34,128,128]{2,1,0:T(8,128)(2,1)S(1)}) custom-call(s32[8]{0:T(128)} %left_ref.1, s32[8]{0:T(128)} %right_ref.1, bf16[8,16,16]{2,1,0:T(8,128)(2,1)} %terms_ref.1, bf16[34,8,128,128]{3,2,1,0:T(8,128)(2,1)} %refs_10_.1), custom_call_target="tpu_custom_call" | custom-call | tf_op jit(solution)/shard_map/ready/pallas_call | solution.py:55
  2.1 0.5 %collective-permute-start = (bf16[8,16,128]{2,1,0:T(8,128)(2,1)S(1)}, bf16[8,16,128]{2,1,0:T(8,128)(2,1)S(1)}, u32[]{:S(2)}, u32[]{:S(2)}) collective-permute-start(bf16[8,16,128]{2,1,0:T(8,128)(2,1)S(1)} %get-tuple-element.9.refs_0_), channel_id=1, source_target_pairs={{0,8},{8,16},{16,24},{24,0},{1,9},{9,17},{17,25},{25,1},{2,10},{10... | collective-permute-start | bytes 98312 | tf_op jit(solution)/shard_map/ppermute | solution.py:29
  2.6 2.6 %collective-permute-start.1 = (bf16[8,16,128]{2,1,0:T(8,128)(2,1)S(1)}, bf16[8,16,128]{2,1,0:T(8,128)(2,1)S(1)}, u32[]{:S(2)}, u32[]{:S(2)}) collective-permute-start(bf16[8,16,128]{2,1,0:T(8,128)(2,1)S(1)} %get-tuple-element.9.refs_0_), channel_id=1, source_target_pairs={{0,16},{8,24},{16,0},{24,8},{1,17},{9,25},{17,1},{25,9},{2,18},{10... | collective-permute-start | bytes 98312 | tf_op jit(solution)/shard_map/ppermute | solution.py:29
  5.2 1.4 %collective-permute-start.2 = (bf16[8,16,128]{2,1,0:T(8,128)(2,1)S(1)}, bf16[8,16,128]{2,1,0:T(8,128)(2,1)S(1)}, u32[]{:S(2)}, u32[]{:S(2)}) collective-permute-start(bf16[8,16,128]{2,1,0:T(8,128)(2,1)S(1)} %get-tuple-element.9.refs_0_), channel_id=1, source_target_pairs={{0,24},{8,0},{16,8},{24,16},{1,25},{9,1},{17,9},{25,17},{2,26},{10... | collective-permute-start | bytes 98312 | tf_op jit(solution)/shard_map/ppermute | solution.py:29
  6.5 3.5 %collective-permute-start.3 = (bf16[34,128,128]{2,1,0:T(8,128)(2,1)S(1)}, bf16[34,128,128]{2,1,0:T(8,128)(2,1)S(1)}, u32[]{:S(2)}, u32[]{:S(2)}) collective-permute-start(bf16[34,128,128]{2,1,0:T(8,128)(2,1)S(1)} %get-tuple-element.10), channel_id=1, source_target_pairs={{0,1},{1,2},{2,3},{3,4},{4,5},{5,6},{6,7},{16,17},{17,18},{18,19},... | collective-permute-start | bytes 3342344 | tf_op jit(solution)/shard_map/ppermute | solution.py:290
  10.0 0.0 collective-permute-done.refs_1_
  10.0 0.0 collective-permute-done.1.refs_2_
  10.0 0.0 collective-permute-done.2.refs_3_
  10.0 23.7 %inner_blocks.1.refs_6_ = bf16[8,4,128,128]{3,2,1,0:T(8,128)(2,1)} custom-call(bf16[8,16,128]{2,1,0:T(8,128)(2,1)S(1)} %get-tuple-element.9.refs_0_, bf16[8,16,128]{2,1,0:T(8,128)(2,1)S(1)} %collective-permute-done.refs_1_, bf16[8,16,128]{2,1,0:T(8,128)(2,1)S(1)} %collective-permute-done.1.refs_2_, bf16[8,16,128]{2,1,0:T(8,128)(2,1)S(1)} %collective-permute-done.2.refs_3_, ...), custom_call_target="tpu_custom_call" | custom-call | flops 12884901888 | bytes 19529728 | tf_op jit(solution)/shard_map/inner_blocks/pallas_call | solution.py:258
  33.7 0.2 collective-permute-done.3.refs_7_
  33.9 9.5 %edge_block.1 = (bf16[8,4,128,128]{3,2,1,0:T(8,128)(2,1)}, bf16[4,128,128]{2,1,0:T(8,128)(2,1)S(1)}) custom-call(bf16[8,16,128]{2,1,0:T(8,128)(2,1)S(1)} %get-tuple-element.9.refs_0_, bf16[8,16,128]{2,1,0:T(8,128)(2,1)S(1)} %collective-permute-done.refs_1_, bf16[8,16,128]{2,1,0:T(8,128)(2,1)S(1)} %collective-permute-done.1.refs_2_, ...), custom_call_target="tpu_custom_call", output_to_operand_aliasing={{0}: (6, {})} | custom-call | flops 4294967296 | bytes 5242880 | tf_op jit(solution)/shard_map/edge_block/pallas_call | solution.py:258
  43.4 0.1 collective-permute-start.4
  43.5 1.3 %collective-permute-done.4 = bf16[4,128,128]{2,1,0:T(8,128)(2,1)S(1)} collective-permute-done((bf16[4,128,128]{2,1,0:T(8,128)(2,1)S(1)}, bf16[4,128,128]{2,1,0:T(8,128)(2,1)S(1)}, u32[]{:S(2)}, u32[]{:S(2)}) %collective-permute-start.4) | collective-permute-done | bytes 131104 | tf_op jit(solution)/shard_map/ppermute | solution.py:295
  44.9 0.7 %bitcast_dynamic-update-slice_fusion = bf16[8,4,128,128]{3,2,1,0:T(8,128)(2,1)} fusion(bf16[8,4,128,128]{3,2,1,0:T(8,128)(2,1)} %get-tuple-element.11, s32[]{:T(128)S(6)} %select_n.3, bf16[4,128,128]{2,1,0:T(8,128)(2,1)S(1)} %collective-permute-done.4), kind=kLoop, calls=%fused_computation | loop fusion | bytes 262148 | tf_op jit(solution)/shard_map/dynamic_update_slice | solution.py:296
Async XLA Ops:
  2.1 8.0 %collective-permute-start = (bf16[8,16,128]{2,1,0:T(8,128)(2,1)S(1)}, bf16[8,16,128]{2,1,0:T(8,128)(2,1)S(1)}, u32[]{:S(2)}, u32[]{:S(2)}) collective-permute-start(bf16[8,16,128]{2,1,0:T(8,128)(2,1)S(1)} %get-tuple-element.9.refs_0_), channel_id=1, source_target_pairs={{0,8},{8,16},{16,24},{24,0},{1,9},{9,17},{17,25},{25,1},{2,10},{10... | collective-permute-start | bytes 98312 | tf_op jit(solution)/shard_map/ppermute | solution.py:29
  2.6 7.5 %collective-permute-start.1 = (bf16[8,16,128]{2,1,0:T(8,128)(2,1)S(1)}, bf16[8,16,128]{2,1,0:T(8,128)(2,1)S(1)}, u32[]{:S(2)}, u32[]{:S(2)}) collective-permute-start(bf16[8,16,128]{2,1,0:T(8,128)(2,1)S(1)} %get-tuple-element.9.refs_0_), channel_id=1, source_target_pairs={{0,16},{8,24},{16,0},{24,8},{1,17},{9,25},{17,1},{25,9},{2,18},{10... | collective-permute-start | bytes 98312 | tf_op jit(solution)/shard_map/ppermute | solution.py:29
  5.2 4.9 %collective-permute-start.2 = (bf16[8,16,128]{2,1,0:T(8,128)(2,1)S(1)}, bf16[8,16,128]{2,1,0:T(8,128)(2,1)S(1)}, u32[]{:S(2)}, u32[]{:S(2)}) collective-permute-start(bf16[8,16,128]{2,1,0:T(8,128)(2,1)S(1)} %get-tuple-element.9.refs_0_), channel_id=1, source_target_pairs={{0,24},{8,0},{16,8},{24,16},{1,25},{9,1},{17,9},{25,17},{2,26},{10... | collective-permute-start | bytes 98312 | tf_op jit(solution)/shard_map/ppermute | solution.py:29
  6.5 27.4 %collective-permute-start.3 = (bf16[34,128,128]{2,1,0:T(8,128)(2,1)S(1)}, bf16[34,128,128]{2,1,0:T(8,128)(2,1)S(1)}, u32[]{:S(2)}, u32[]{:S(2)}) collective-permute-start(bf16[34,128,128]{2,1,0:T(8,128)(2,1)S(1)} %get-tuple-element.10), channel_id=1, source_target_pairs={{0,1},{1,2},{2,3},{3,4},{4,5},{5,6},{6,7},{16,17},{17,18},{18,19},... | collective-permute-start | bytes 3342344 | tf_op jit(solution)/shard_map/ppermute | solution.py:290
  43.4 1.4 %collective-permute-start.4 = (bf16[4,128,128]{2,1,0:T(8,128)(2,1)S(1)}, bf16[4,128,128]{2,1,0:T(8,128)(2,1)S(1)}, u32[]{:S(2)}, u32[]{:S(2)}) collective-permute-start(bf16[4,128,128]{2,1,0:T(8,128)(2,1)S(1)} %get-tuple-element.12), channel_id=1, source_target_pairs={{0,8},{8,0},{16,24},{24,16},{1,9},{9,1},{17,25},{25,17},{2,10},{10... | collective-permute-start | bytes 393224 | tf_op jit(solution)/shard_map/ppermute | solution.py:295

commit v3 on v2

--- a/solution.py
+++ b/solution.py
@@ -11,6 +11,7 @@
 BF, F32, I32 = jnp.bfloat16, jnp.float32, jnp.int32
 ROWS = 16
 LANES = 128
+CUTS = 4
 SPARE_VMEM = 12 * 2**20
 MOST_VMEM = 60 * 2**20
 
@@ -29,12 +30,16 @@
     return [mine, *(lax.ppermute(mine, axis, pairs) for pairs in turns)]
 
 
-def ready_kernel(left_ref, right_ref, terms_ref, env_ref, packed_ref, sent_ref, sem):
+def ready_kernel(left_ref, right_ref, terms_ref, env_ref, packed_ref, sent_ref, sems):
     terms, states, _ = terms_ref.shape
     core = lax.rem(lax.axis_index("mpo"), 2)
     edge = (1 - core) * (env_ref.shape[1] - 1)
-    copy = pltpu.make_async_copy(env_ref.at[:, edge], sent_ref, sem)
-    copy.start()
+    share = -(-sent_ref.shape[0] // CUTS)
+    copies = []
+    for cut in range(CUTS):
+        span = pl.ds(cut * share, min(share, sent_ref.shape[0] - cut * share))
+        copies.append(pltpu.make_async_copy(env_ref.at[span, edge], sent_ref.at[span], sems.at[cut]))
+        copies[-1].start()
     packed_ref[...] = jnp.zeros_like(packed_ref)
     packed_ref[:, :, :states] = terms_ref[...]
     lane = iota((states, LANES), 1)
@@ -43,7 +48,8 @@
         row = jnp.where(lane == states, left_ref[t].astype(F32), row)
         row = jnp.where(lane == states + 1, right_ref[t].astype(F32), row)
         packed_ref[t] = row.astype(BF)
-    copy.wait()
+    for copy in copies:
+        copy.wait()
 
 
 def ready(term_left, term_right, mpo_terms, right_env):
@@ -60,7 +66,7 @@
         ],
         in_specs=[smem, smem, vmem, anyw],
         out_specs=[vmem, vmem],
-        scratch_shapes=[pltpu.SemaphoreType.DMA],
+        scratch_shapes=[pltpu.SemaphoreType.DMA((CUTS,))],
         name="ready",
     )(term_left, term_right, mpo_terms, right_env)
 
@@ -88,11 +94,11 @@
     two, left, right, out = (refs.pop(0) for _ in range(4))
     if edge:
         passed = refs.pop(0)
-    packed, spread, clean, lefts, rights, mixed, joined, result, wide, index, shifts, sizes, sems = refs
+    spread, keeps, clean, lefts, rights, mixed, joined, result, wide, index, shifts, sizes, sems = refs
 
     blocks, states, depth, _ = two.shape
-    terms = packed.shape[0]
-    share = terms // len(pieces)
+    share = pieces[0].shape[0]
+    terms = share * len(pieces)
     me = lax.axis_index("mpo")
     core = lax.rem(me, 2)
     first = lax.axis_index("blk") * blocks
@@ -119,72 +125,57 @@
         return pltpu.make_async_copy(wide, index, sems.at[3, 0])
 
     small = [
-        pltpu.make_async_copy(piece, packed.at[pl.ds(n * share, share)], sems.at[5, n])
-        for n, piece in enumerate(pieces)
-    ] + [pltpu.make_async_copy(a, b, sems.at[6, n]) for n, (a, b) in enumerate(zip(numbers, (shifts, sizes)))]
+        pltpu.make_async_copy(a, b, sems.at[5, n]) for n, (a, b) in enumerate(zip(numbers, (shifts, sizes)))
+    ]
     for copy in small:
         copy.start()
     two_copy(0).start()
-
-    def live(n, p=None):
-        j = first + place(n) + (0 if p is None else shifts[p])
-        return jnp.where((j >= 0) & (j < total), sizes[jnp.clip(j, 0, total - 1)], 0)
-
-    def wipe(n):
-        keep_rows = jnp.where(iota((depth, depth), 0) < live(n), 1.0, 0.0).astype(BF)
-        lane = iota((ROWS, depth), 1)
-        for q in range(states):
-            keep_cols = jnp.where(lane < live(n, q), 1.0, 0.0).astype(BF)
-            block = clean[n, q].reshape(depth // ROWS, ROWS, depth) * keep_cols[None]
-            clean[n, q] = block.reshape(depth, depth) * keep_rows
-
+    for slot in range(3):
+        right_copy(slot).start()
+    left_copy(0).start()
+    for n, piece in enumerate(pieces):
+        wide[n * share : (n + 1) * share, :] = piece[:, 0, :].astype(F32).astype(I32)
+    index_copy().start()
+    for n, piece in enumerate(pieces):
+        spread_terms(piece, spread.at[pl.ds(n * share * own * ROWS, share * own * ROWS)], own, mine)
     for copy in small:
         copy.wait()
-    wide[...] = packed[:, 0, :].astype(F32).astype(I32)
-    index_copy().start()
-    spread_terms(packed, spread, own, mine)
+
+    def live(slot):
+        j = first + place(0) - 1 + slot
+        return jnp.where((j >= 0) & (j < total), sizes[jnp.clip(j, 0, total - 1)], 0)
+
+    for slot in range(count + 2):
+        keeps[slot] = jnp.where(iota((ROWS, depth), 1) < live(slot), 1.0, 0.0).astype(BF)
     two_copy(0).wait()
-    wipe(0)
-    for n in range(count):
-        for slot in (0, 1, 2) if n == 0 else (n + 2,):
-            right_copy(slot).start()
+    for n in range(1, count):
+        two_copy(n).start()
+        right_copy(n + 2).start()
         left_copy(n).start()
-        if n + 1 < count:
-            two_copy(n + 1).start()
-    index_copy().wait()
-
-    def apply(n):
-        i = place(n)
+
+    def apply(n, leading):
+        size = live(n + 1)
+        if not leading:
+            two_copy(n).wait()
+            right_copy(n + 2).wait()
+            left_copy(n).wait()
 
         for h in range(depth // (2 * ROWS)):
             spans = [slice((2 * h + u) * ROWS, (2 * h + u + 1) * ROWS) for u in range(2)]
-            both = jnp.concatenate(
-                [clean[n, :, s, :].reshape(states * ROWS, depth) for s in spans], axis=1
-            )
+            both = []
+            for s in spans:
+                keep_rows = jnp.where(iota((ROWS, depth), 0) + s.start < size, 1.0, 0.0).astype(BF)
+                both.append([clean[n, q, s, :] * keeps[n + 1 + shifts[q]] * keep_rows for q in range(states)])
+            both = jnp.concatenate([jnp.concatenate(tiles, axis=0) for tiles in both], axis=1)
             part = dot(spread[...], both).astype(BF).reshape(terms, own, ROWS, 2 * depth)
             for u in range(2):
                 mixed[:, :, spans[u], :] = part[:, :, :, u * depth : (u + 1) * depth]
 
-        if edge:
+        if leading:
+            index_copy().wait()
             for slot in range(3):
                 right_copy(slot).wait()
-        else:
-
-            @pl.when(n == 0)
-            def _():
-                right_copy(0).wait()
-                right_copy(1).wait()
-
-            right_copy(n + 2).wait()
-        if not edge:
-            later = jnp.minimum(n + 1, count - 1)
-
-            @pl.when(n + 1 < count)
-            def _():
-                two_copy(n + 1).wait()
-
-            wipe(later)
-        slot_of = [(1 if edge else n + 1) + shifts[mine + p] for p in range(own)]
+        slot_of = [n + 1 + shifts[mine + p] for p in range(own)]
         for t in range(terms):
             bond = index[t, states + 1]
             for p in range(own):
@@ -192,16 +183,17 @@
                     mixed[t, p], rights[slot_of[p], bond]
                 ).astype(BF)
 
-        left_copy(n).wait()
+        if leading:
+            left_copy(n).wait()
         row = jnp.concatenate([lefts[n, index[t, states]] for t in range(terms)], axis=1)
         summed = dot(row, joined[...].reshape(terms * depth, own * depth))
-        rows, cols = iota((depth, depth), 0), iota((depth, depth), 1)
+        keep_rows = jnp.where(iota((depth, depth), 0) < size, 1.0, 0.0)
         for p in range(own):
-            keep = (rows < live(n)) & (cols < live(n, mine + p))
-            result[n, p] = jnp.where(keep, summed[:, p * depth : (p + 1) * depth], 0.0).astype(BF)
+            keep = keep_rows * keeps[slot_of[p], :1, :].astype(F32)
+            result[n, p] = (summed[:, p * depth : (p + 1) * depth] * keep).astype(BF)
 
     if edge:
-        apply(0)
+        apply(0, True)
         half = own // 2
         ours = pltpu.make_async_copy(
             result.at[0, pl.ds(core * half, half)], out.at[place(0)], sems.at[0, 0]
@@ -218,9 +210,12 @@
         def out_copy(n):
             return pltpu.make_async_copy(result.at[n], out.at[place(n)], sems.at[4, n])
 
-        @pl.loop(0, count)
+        apply(0, True)
+        out_copy(0).start()
+
+        @pl.loop(1, count)
         def _(n):
-            apply(n)
+            apply(n, False)
             out_copy(n).start()
 
         for n in range(count):
@@ -233,6 +228,7 @@
     count = 1 if edge else blocks - 2
     slots = count + 2
     anyw = pl.BlockSpec(memory_space=pl.ANY)
+    vmem = pl.BlockSpec(memory_space=pltpu.VMEM)
     near = functools.partial(pltpu.with_memory_space_constraint, memory_space=pltpu.VMEM)
     far = functools.partial(pltpu.with_memory_space_constraint, memory_space=pltpu.HBM)
     operands = [*map(near, pieces), far(shifts), far(sizes)]
@@ -243,8 +239,8 @@
     if edge:
         out_shapes.append(jax.ShapeDtypeStruct((kept, depth, depth), BF))
     buffers = [
-        (terms, states, LANES),
         (terms * own * ROWS, states * ROWS),
+        (slots, ROWS, depth),
         (count, states, depth, depth),
         (count, bonds, depth, depth),
         (slots, bonds, depth, depth),
@@ -253,12 +249,10 @@
         (count, own, depth, depth),
     ]
     held = sum(2 * math.prod(shape) for shape in buffers)
-    flops = 2 * count * terms * own * depth**2 * (2 * depth + states * ROWS)
-    moved = 2 * depth**2 * (count * (states + bonds + own) + slots * bonds)
     return pl.pallas_call(
         functools.partial(block_kernel, edge, count, own, total),
         out_shape=out_shapes,
-        in_specs=[anyw] * len(operands),
+        in_specs=[vmem] * len(pieces) + [anyw] * (len(operands) - len(pieces)),
         out_specs=[anyw] * len(out_shapes),
         input_output_aliases={len(pieces) + 2: 0} if edge else {},
         scratch_shapes=[
@@ -267,10 +261,9 @@
             pltpu.SMEM((terms, LANES), I32),
             pltpu.SMEM(shifts.shape, I32),
             pltpu.SMEM(sizes.shape, I32),
-            pltpu.SemaphoreType.DMA((7, max(slots, len(pieces)))),
+            pltpu.SemaphoreType.DMA((6, slots)),
         ],
         compiler_params=pltpu.CompilerParams(vmem_limit_bytes=min(held + SPARE_VMEM, MOST_VMEM)),
-        cost_estimate=pl.CostEstimate(flops=flops, bytes_accessed=moved, transcendentals=0),
         name="edge_block" if edge else "inner_blocks",
     )(*operands)
 
@@ -282,12 +275,11 @@
     core = lax.rem(lax.axis_index("mpo"), 2)
 
     packed, sent = ready(term_left, term_right, mpo_terms, right_env)
-    pieces = gathered(packed, "mpo")
-
     place = lambda m, b: m * count + b
     up = [(place(m, b), place(m, b + 1)) for m in range(0, groups, 2) for b in range(count - 1)]
     down = [(place(m, b + 1), place(m, b)) for m in range(1, groups, 2) for b in range(count - 1)]
     halo = lax.ppermute(sent, ("mpo", "blk"), up + down)
+    pieces = gathered(packed, "mpo")
 
     arrays = (pieces, shifts, block_sizes, two_site, left_env, right_env)
     (done,) = apply_blocks(False, *arrays, own, total)

time: 45.8 us -> 43.9 us (0.959)
  Pallas kernels: 35.2 us -> 31.8 us
  waiting for transfers between devices: 1.54 us -> 2.59 us
  starting transfers between devices: 8.01 us -> 8.63 us
    pallas_call x2, Pallas kernels: 33.2 us -> 29.8 us  [apply_blocks(): pl.pallas_call(functools.partial(block_kernel, edge, count, own, total),...]
    ppermute x3, waiting for transfers between devices: 0.01 us -> 1.6 us  [gathered(): return [mine, *(lax.ppermute(mine, axis, pairs) for pairs in turns)]]
    ppermute x1, starting transfers between devices: 3.45 us -> 4.91 us  [body(): halo = lax.ppermute(sent, ('mpo', 'blk'), up + down)]
    ppermute x3, starting transfers between devices: 4.48 us -> 3.03 us  [gathered(): return [mine, *(lax.ppermute(mine, axis, pairs) for pairs in turns)]]
    ppermute x1, starting transfers between devices: 0.07 us -> 0.68 us  [body(): passed = lax.ppermute(passed, 'mpo', [(m, m ^ 1) for m in range(groups)])]
  transfers between devices with their start and end apart: 5 -> 5, of which waited for: 2 -> 4; matrix products, arithmetic and copies ran while one was open for 0% -> 0% of each run, Pallas kernels for 52% -> 49%
where the time goes in v3:
time: 43.9 us; the launch traced here: 43.7 us
  Pallas kernels  31.8 us (72%)
  starting transfers between devices  8.63 us (20%)
  waiting for transfers between devices  2.59 us (6%)
  local copies, waits for them, and re-layouts  0.66 us (2%)
    pallas_call x2, Pallas kernels, apply_blocks(): pl.pallas_call(functools.partial(block_kernel, edge, count, own, total),...  29.8 us
    ppermute x1, starting transfers between devices, body(): halo = lax.ppermute(sent, ('mpo', 'blk'), up + down)  4.91 us
    ppermute x3, starting transfers between devices, gathered(): return [mine, *(lax.ppermute(mine, axis, pairs) for pairs in turns)]  3.03 us
    pallas_call x1, Pallas kernels, ready(): pl.pallas_call(ready_kernel, out_shape=[pltpu.VMEM((terms, states, LANES)...  2.03 us
    ppermute x3, waiting for transfers between devices, gathered(): return [mine, *(lax.ppermute(mine, axis, pairs) for pairs in turns)]  1.6 us
    ppermute x1, waiting for transfers between devices, body(): passed = lax.ppermute(passed, 'mpo', [(m, m ^ 1) for m in range(groups)])  0.99 us
  transfers between devices with their start and end apart: 5, of which 4 were waited for; matrix products, arithmetic and copies ran while one was open for 0% of the time, Pallas kernels for 49%

profile of v3, /device:TPU:0, one launch (start us, length us, event | category | flops | bytes accessed | tf_op | source)
XLA Modules:
  0.0 43.7 jit_solution(10862800003904323904)
XLA Ops:
  0.0 2.0 %ready.1 = (bf16[8,16,128]{2,1,0:T(8,128)(2,1)S(1)}, bf16[34,128,128]{2,1,0:T(8,128)(2,1)S(1)}) custom-call(s32[8]{0:T(128)} %left_ref.1, s32[8]{0:T(128)} %right_ref.1, bf16[8,16,16]{2,1,0:T(8,128)(2,1)} %terms_ref.1, bf16[34,8,128,128]{3,2,1,0:T(8,128)(2,1)} %refs_10_.1), custom_call_target="tpu_custom_call" | custom-call | tf_op jit(solution)/shard_map/ready/pallas_call | solution.py:61
  2.0 4.9 %collective-permute-start.3 = (bf16[34,128,128]{2,1,0:T(8,128)(2,1)S(1)}, bf16[34,128,128]{2,1,0:T(8,128)(2,1)S(1)}, u32[]{:S(2)}, u32[]{:S(2)}) collective-permute-start(bf16[34,128,128]{2,1,0:T(8,128)(2,1)S(1)} %get-tuple-element.10), channel_id=1, source_target_pairs={{0,1},{1,2},{2,3},{3,4},{4,5},{5,6},{6,7},{16,17},{17,18},{18,19},... | collective-permute-start | bytes 3342344 | tf_op jit(solution)/shard_map/ppermute | solution.py:281
  7.0 0.1 collective-permute-start
  7.0 1.6 %collective-permute-start.1 = (bf16[8,16,128]{2,1,0:T(8,128)(2,1)S(1)}, bf16[8,16,128]{2,1,0:T(8,128)(2,1)S(1)}, u32[]{:S(2)}, u32[]{:S(2)}) collective-permute-start(bf16[8,16,128]{2,1,0:T(8,128)(2,1)S(1)} %get-tuple-element.9.refs_0_), channel_id=1, source_target_pairs={{0,16},{8,24},{16,0},{24,8},{1,17},{9,25},{17,1},{25,9},{2,18},{10... | collective-permute-start | bytes 98312 | tf_op jit(solution)/shard_map/ppermute | solution.py:30
  8.6 1.4 %collective-permute-start.2 = (bf16[8,16,128]{2,1,0:T(8,128)(2,1)S(1)}, bf16[8,16,128]{2,1,0:T(8,128)(2,1)S(1)}, u32[]{:S(2)}, u32[]{:S(2)}) collective-permute-start(bf16[8,16,128]{2,1,0:T(8,128)(2,1)S(1)} %get-tuple-element.9.refs_0_), channel_id=1, source_target_pairs={{0,24},{8,0},{16,8},{24,16},{1,25},{9,1},{17,9},{25,17},{2,26},{10... | collective-permute-start | bytes 98312 | tf_op jit(solution)/shard_map/ppermute | solution.py:30
  10.0 0.4 collective-permute-done.refs_1_
  10.3 0.7 %collective-permute-done.1.refs_2_ = bf16[8,16,128]{2,1,0:T(8,128)(2,1)S(1)} collective-permute-done((bf16[8,16,128]{2,1,0:T(8,128)(2,1)S(1)}, bf16[8,16,128]{2,1,0:T(8,128)(2,1)S(1)}, u32[]{:S(2)}, u32[]{:S(2)}) %collective-permute-start.1) | collective-permute-done | bytes 32800 | tf_op jit(solution)/shard_map/ppermute | solution.py:30
  11.0 0.6 %collective-permute-done.2.refs_3_ = bf16[8,16,128]{2,1,0:T(8,128)(2,1)S(1)} collective-permute-done((bf16[8,16,128]{2,1,0:T(8,128)(2,1)S(1)}, bf16[8,16,128]{2,1,0:T(8,128)(2,1)S(1)}, u32[]{:S(2)}, u32[]{:S(2)}) %collective-permute-start.2) | collective-permute-done | bytes 32800 | tf_op jit(solution)/shard_map/ppermute | solution.py:30
  11.6 21.3 %inner_blocks.1.refs_6_ = bf16[8,4,128,128]{3,2,1,0:T(8,128)(2,1)} custom-call(bf16[8,16,128]{2,1,0:T(8,128)(2,1)S(1)} %get-tuple-element.9.refs_0_, bf16[8,16,128]{2,1,0:T(8,128)(2,1)S(1)} %collective-permute-done.refs_1_, bf16[8,16,128]{2,1,0:T(8,128)(2,1)S(1)} %collective-permute-done.1.refs_2_, bf16[8,16,128]{2,1,0:T(8,128)(2,1)S(1)} %collective-permute-done.2.refs_3_, ...), custom_call_target="tpu_custom_call" | custom-call | tf_op jit(solution)/shard_map/inner_blocks/pallas_call | solution.py:252
  32.9 0.0 collective-permute-done.3.refs_7_
  32.9 8.5 %edge_block.1 = (bf16[8,4,128,128]{3,2,1,0:T(8,128)(2,1)}, bf16[4,128,128]{2,1,0:T(8,128)(2,1)S(1)}) custom-call(bf16[8,16,128]{2,1,0:T(8,128)(2,1)S(1)} %get-tuple-element.9.refs_0_, bf16[8,16,128]{2,1,0:T(8,128)(2,1)S(1)} %collective-permute-done.refs_1_, bf16[8,16,128]{2,1,0:T(8,128)(2,1)S(1)} %collective-permute-done.1.refs_2_, ...), custom_call_target="tpu_custom_call", output_to_operand_aliasing={{0}: (6, {})} | custom-call | tf_op jit(solution)/shard_map/edge_block/pallas_call | solution.py:252
  41.4 0.7 %collective-permute-start.4 = (bf16[4,128,128]{2,1,0:T(8,128)(2,1)S(1)}, bf16[4,128,128]{2,1,0:T(8,128)(2,1)S(1)}, u32[]{:S(2)}, u32[]{:S(2)}) collective-permute-start(bf16[4,128,128]{2,1,0:T(8,128)(2,1)S(1)} %get-tuple-element.12), channel_id=1, source_target_pairs={{0,8},{8,0},{16,24},{24,16},{1,9},{9,1},{17,25},{25,17},{2,10},{10... | collective-permute-start | bytes 393224 | tf_op jit(solution)/shard_map/ppermute | solution.py:287
  42.1 1.0 %collective-permute-done.4 = bf16[4,128,128]{2,1,0:T(8,128)(2,1)S(1)} collective-permute-done((bf16[4,128,128]{2,1,0:T(8,128)(2,1)S(1)}, bf16[4,128,128]{2,1,0:T(8,128)(2,1)S(1)}, u32[]{:S(2)}, u32[]{:S(2)}) %collective-permute-start.4) | collective-permute-done | bytes 131104 | tf_op jit(solution)/shard_map/ppermute | solution.py:287
  43.1 0.7 %bitcast_dynamic-update-slice_fusion = bf16[8,4,128,128]{3,2,1,0:T(8,128)(2,1)} fusion(bf16[8,4,128,128]{3,2,1,0:T(8,128)(2,1)} %get-tuple-element.11, s32[]{:T(128)S(6)} %select_n.3, bf16[4,128,128]{2,1,0:T(8,128)(2,1)S(1)} %collective-permute-done.4), kind=kLoop, calls=%fused_computation | loop fusion | bytes 262148 | tf_op jit(solution)/shard_map/dynamic_update_slice | solution.py:288
Async XLA Ops:
  2.0 30.8 %collective-permute-start.3 = (bf16[34,128,128]{2,1,0:T(8,128)(2,1)S(1)}, bf16[34,128,128]{2,1,0:T(8,128)(2,1)S(1)}, u32[]{:S(2)}, u32[]{:S(2)}) collective-permute-start(bf16[34,128,128]{2,1,0:T(8,128)(2,1)S(1)} %get-tuple-element.10), channel_id=1, source_target_pairs={{0,1},{1,2},{2,3},{3,4},{4,5},{5,6},{6,7},{16,17},{17,18},{18,19},... | collective-permute-start | bytes 3342344 | tf_op jit(solution)/shard_map/ppermute | solution.py:281
  7.0 3.4 %collective-permute-start = (bf16[8,16,128]{2,1,0:T(8,128)(2,1)S(1)}, bf16[8,16,128]{2,1,0:T(8,128)(2,1)S(1)}, u32[]{:S(2)}, u32[]{:S(2)}) collective-permute-start(bf16[8,16,128]{2,1,0:T(8,128)(2,1)S(1)} %get-tuple-element.9.refs_0_), channel_id=1, source_target_pairs={{0,8},{8,16},{16,24},{24,0},{1,9},{9,17},{17,25},{25,1},{2,10},{10... | collective-permute-start | bytes 98312 | tf_op jit(solution)/shard_map/ppermute | solution.py:30
  7.0 4.0 %collective-permute-start.1 = (bf16[8,16,128]{2,1,0:T(8,128)(2,1)S(1)}, bf16[8,16,128]{2,1,0:T(8,128)(2,1)S(1)}, u32[]{:S(2)}, u32[]{:S(2)}) collective-permute-start(bf16[8,16,128]{2,1,0:T(8,128)(2,1)S(1)} %get-tuple-element.9.refs_0_), channel_id=1, source_target_pairs={{0,16},{8,24},{16,0},{24,8},{1,17},{9,25},{17,1},{25,9},{2,18},{10... | collective-permute-start | bytes 98312 | tf_op jit(solution)/shard_map/ppermute | solution.py:30
  8.6 3.0 %collective-permute-start.2 = (bf16[8,16,128]{2,1,0:T(8,128)(2,1)S(1)}, bf16[8,16,128]{2,1,0:T(8,128)(2,1)S(1)}, u32[]{:S(2)}, u32[]{:S(2)}) collective-permute-start(bf16[8,16,128]{2,1,0:T(8,128)(2,1)S(1)} %get-tuple-element.9.refs_0_), channel_id=1, source_target_pairs={{0,24},{8,0},{16,8},{24,16},{1,25},{9,1},{17,9},{25,17},{2,26},{10... | collective-permute-start | bytes 98312 | tf_op jit(solution)/shard_map/ppermute | solution.py:30
  41.4 1.7 %collective-permute-start.4 = (bf16[4,128,128]{2,1,0:T(8,128)(2,1)S(1)}, bf16[4,128,128]{2,1,0:T(8,128)(2,1)S(1)}, u32[]{:S(2)}, u32[]{:S(2)}) collective-permute-start(bf16[4,128,128]{2,1,0:T(8,128)(2,1)S(1)} %get-tuple-element.12), channel_id=1, source_target_pairs={{0,8},{8,0},{16,24},{24,16},{1,9},{9,1},{17,25},{25,17},{2,10},{10... | collective-permute-start | bytes 393224 | tf_op jit(solution)/shard_map/ppermute | solution.py:287

commit v4 on v3

--- a/solution.py
+++ b/solution.py
@@ -30,8 +30,14 @@
     return [mine, *(lax.ppermute(mine, axis, pairs) for pairs in turns)]
 
 
-def ready_kernel(left_ref, right_ref, terms_ref, env_ref, packed_ref, sent_ref, sems):
+def ready_kernel(left_hbm, right_hbm, terms_hbm, env_ref, packed_ref, sent_ref, left_ref, right_ref, terms_ref, sems):
     terms, states, _ = terms_ref.shape
+    small = [
+        pltpu.make_async_copy(a, b, sems.at[CUTS + n])
+        for n, (a, b) in enumerate(((left_hbm, left_ref), (right_hbm, right_ref), (terms_hbm, terms_ref)))
+    ]
+    for copy in small:
+        copy.start()
     core = lax.rem(lax.axis_index("mpo"), 2)
     edge = (1 - core) * (env_ref.shape[1] - 1)
     share = -(-sent_ref.shape[0] // CUTS)
@@ -40,6 +46,8 @@
         span = pl.ds(cut * share, min(share, sent_ref.shape[0] - cut * share))
         copies.append(pltpu.make_async_copy(env_ref.at[span, edge], sent_ref.at[span], sems.at[cut]))
         copies[-1].start()
+    for copy in small:
+        copy.wait()
     packed_ref[...] = jnp.zeros_like(packed_ref)
     packed_ref[:, :, :states] = terms_ref[...]
     lane = iota((states, LANES), 1)
@@ -55,7 +63,6 @@
 def ready(term_left, term_right, mpo_terms, right_env):
     terms, states, _ = mpo_terms.shape
     bonds, _, depth, _ = right_env.shape
-    smem = pl.BlockSpec(memory_space=pltpu.SMEM)
     vmem = pl.BlockSpec(memory_space=pltpu.VMEM)
     anyw = pl.BlockSpec(memory_space=pl.ANY)
     return pl.pallas_call(
@@ -64,11 +71,16 @@
             pltpu.VMEM((terms, states, LANES), BF),
             pltpu.VMEM((bonds, depth, depth), BF),
         ],
-        in_specs=[smem, smem, vmem, anyw],
+        in_specs=[anyw] * 4,
         out_specs=[vmem, vmem],
-        scratch_shapes=[pltpu.SemaphoreType.DMA((CUTS,))],
+        scratch_shapes=[
+            pltpu.SMEM((terms,), I32),
+            pltpu.SMEM((terms,), I32),
+            pltpu.VMEM(mpo_terms.shape, BF),
+            pltpu.SemaphoreType.DMA((CUTS + 3,)),
+        ],
         name="ready",
-    )(term_left, term_right, mpo_terms, right_env)
+    )(*(pltpu.with_memory_space_constraint(x, pltpu.HBM) for x in (term_left, term_right, mpo_terms, right_env)))
 
 
 def spread_terms(packed, spread, own, mine):

time: 43.9 us -> 43.2 us (0.984)
  Pallas kernels: 31.8 us -> 31.1 us
    pallas_call x1, Pallas kernels: 2.03 us -> 1.29 us  [ready(): pl.pallas_call(ready_kernel, out_shape=[pltpu.VMEM((terms, states, LANES)...]
where the time goes in v4:
time: 43.2 us; the launch traced here: 43 us
  Pallas kernels  31.1 us (72%)
  starting transfers between devices  8.62 us (20%)
  waiting for transfers between devices  2.59 us (6%)
  local copies, waits for them, and re-layouts  0.66 us (2%)
    pallas_call x2, Pallas kernels, apply_blocks(): pl.pallas_call(functools.partial(block_kernel, edge, count, own, total),...  29.8 us
    ppermute x1, starting transfers between devices, body(): halo = lax.ppermute(sent, ('mpo', 'blk'), up + down)  4.91 us
    ppermute x3, starting transfers between devices, gathered(): return [mine, *(lax.ppermute(mine, axis, pairs) for pairs in turns)]  3.03 us
    ppermute x3, waiting for transfers between devices, gathered(): return [mine, *(lax.ppermute(mine, axis, pairs) for pairs in turns)]  1.6 us
    pallas_call x1, Pallas kernels, ready(): pl.pallas_call(ready_kernel, out_shape=[pltpu.VMEM((terms, states, LANES)...  1.29 us
    ppermute x1, waiting for transfers between devices, body(): passed = lax.ppermute(passed, 'mpo', [(m, m ^ 1) for m in range(groups)])  0.99 us
  transfers between devices with their start and end apart: 5, of which 4 were waited for; matrix products, arithmetic and copies ran while one was open for 0% of the time, Pallas kernels for 49%

profile of v4, /device:TPU:0, one launch (start us, length us, event | category | flops | bytes accessed | tf_op | source)
XLA Modules:
  0.0 43.0 jit_solution(17603376150008551341)
XLA Ops:
  0.0 1.3 %ready.1 = (bf16[8,16,128]{2,1,0:T(8,128)(2,1)S(1)}, bf16[34,128,128]{2,1,0:T(8,128)(2,1)S(1)}) custom-call(s32[8]{0:T(128)} %left_hbm.1, s32[8]{0:T(128)} %right_hbm.1, bf16[8,16,16]{2,1,0:T(8,128)(2,1)} %terms_hbm.1, bf16[34,8,128,128]{3,2,1,0:T(8,128)(2,1)} %refs_10_.1), custom_call_target="tpu_custom_call" | custom-call | tf_op jit(solution)/shard_map/ready/pallas_call | solution.py:68
  1.3 4.9 %collective-permute-start.3 = (bf16[34,128,128]{2,1,0:T(8,128)(2,1)S(1)}, bf16[34,128,128]{2,1,0:T(8,128)(2,1)S(1)}, u32[]{:S(2)}, u32[]{:S(2)}) collective-permute-start(bf16[34,128,128]{2,1,0:T(8,128)(2,1)S(1)} %get-tuple-element.10), channel_id=1, source_target_pairs={{0,1},{1,2},{2,3},{3,4},{4,5},{5,6},{6,7},{16,17},{17,18},{18,19},... | collective-permute-start | bytes 3342344 | tf_op jit(solution)/shard_map/ppermute | solution.py:293
  6.2 0.1 collective-permute-start
  6.3 1.6 %collective-permute-start.1 = (bf16[8,16,128]{2,1,0:T(8,128)(2,1)S(1)}, bf16[8,16,128]{2,1,0:T(8,128)(2,1)S(1)}, u32[]{:S(2)}, u32[]{:S(2)}) collective-permute-start(bf16[8,16,128]{2,1,0:T(8,128)(2,1)S(1)} %get-tuple-element.9.refs_0_), channel_id=1, source_target_pairs={{0,16},{8,24},{16,0},{24,8},{1,17},{9,25},{17,1},{25,9},{2,18},{10... | collective-permute-start | bytes 98312 | tf_op jit(solution)/shard_map/ppermute | solution.py:30
  7.9 1.4 %collective-permute-start.2 = (bf16[8,16,128]{2,1,0:T(8,128)(2,1)S(1)}, bf16[8,16,128]{2,1,0:T(8,128)(2,1)S(1)}, u32[]{:S(2)}, u32[]{:S(2)}) collective-permute-start(bf16[8,16,128]{2,1,0:T(8,128)(2,1)S(1)} %get-tuple-element.9.refs_0_), channel_id=1, source_target_pairs={{0,24},{8,0},{16,8},{24,16},{1,25},{9,1},{17,9},{25,17},{2,26},{10... | collective-permute-start | bytes 98312 | tf_op jit(solution)/shard_map/ppermute | solution.py:30
  9.3 0.4 collective-permute-done.refs_1_
  9.6 0.7 %collective-permute-done.1.refs_2_ = bf16[8,16,128]{2,1,0:T(8,128)(2,1)S(1)} collective-permute-done((bf16[8,16,128]{2,1,0:T(8,128)(2,1)S(1)}, bf16[8,16,128]{2,1,0:T(8,128)(2,1)S(1)}, u32[]{:S(2)}, u32[]{:S(2)}) %collective-permute-start.1) | collective-permute-done | bytes 32800 | tf_op jit(solution)/shard_map/ppermute | solution.py:30
  10.3 0.6 %collective-permute-done.2.refs_3_ = bf16[8,16,128]{2,1,0:T(8,128)(2,1)S(1)} collective-permute-done((bf16[8,16,128]{2,1,0:T(8,128)(2,1)S(1)}, bf16[8,16,128]{2,1,0:T(8,128)(2,1)S(1)}, u32[]{:S(2)}, u32[]{:S(2)}) %collective-permute-start.2) | collective-permute-done | bytes 32800 | tf_op jit(solution)/shard_map/ppermute | solution.py:30
  10.9 21.3 %inner_blocks.1.refs_6_ = bf16[8,4,128,128]{3,2,1,0:T(8,128)(2,1)} custom-call(bf16[8,16,128]{2,1,0:T(8,128)(2,1)S(1)} %get-tuple-element.9.refs_0_, bf16[8,16,128]{2,1,0:T(8,128)(2,1)S(1)} %collective-permute-done.refs_1_, bf16[8,16,128]{2,1,0:T(8,128)(2,1)S(1)} %collective-permute-done.1.refs_2_, bf16[8,16,128]{2,1,0:T(8,128)(2,1)S(1)} %collective-permute-done.2.refs_3_, ...), custom_call_target="tpu_custom_call" | custom-call | tf_op jit(solution)/shard_map/inner_blocks/pallas_call | solution.py:264
  32.1 0.0 collective-permute-done.3.refs_7_
  32.1 8.5 %edge_block.1 = (bf16[8,4,128,128]{3,2,1,0:T(8,128)(2,1)}, bf16[4,128,128]{2,1,0:T(8,128)(2,1)S(1)}) custom-call(bf16[8,16,128]{2,1,0:T(8,128)(2,1)S(1)} %get-tuple-element.9.refs_0_, bf16[8,16,128]{2,1,0:T(8,128)(2,1)S(1)} %collective-permute-done.refs_1_, bf16[8,16,128]{2,1,0:T(8,128)(2,1)S(1)} %collective-permute-done.1.refs_2_, ...), custom_call_target="tpu_custom_call", output_to_operand_aliasing={{0}: (6, {})} | custom-call | tf_op jit(solution)/shard_map/edge_block/pallas_call | solution.py:264
  40.7 0.7 %collective-permute-start.4 = (bf16[4,128,128]{2,1,0:T(8,128)(2,1)S(1)}, bf16[4,128,128]{2,1,0:T(8,128)(2,1)S(1)}, u32[]{:S(2)}, u32[]{:S(2)}) collective-permute-start(bf16[4,128,128]{2,1,0:T(8,128)(2,1)S(1)} %get-tuple-element.12), channel_id=1, source_target_pairs={{0,8},{8,0},{16,24},{24,16},{1,9},{9,1},{17,25},{25,17},{2,10},{10... | collective-permute-start | bytes 393224 | tf_op jit(solution)/shard_map/ppermute | solution.py:299
  41.3 1.0 %collective-permute-done.4 = bf16[4,128,128]{2,1,0:T(8,128)(2,1)S(1)} collective-permute-done((bf16[4,128,128]{2,1,0:T(8,128)(2,1)S(1)}, bf16[4,128,128]{2,1,0:T(8,128)(2,1)S(1)}, u32[]{:S(2)}, u32[]{:S(2)}) %collective-permute-start.4) | collective-permute-done | bytes 131104 | tf_op jit(solution)/shard_map/ppermute | solution.py:299
  42.3 0.7 %bitcast_dynamic-update-slice_fusion = bf16[8,4,128,128]{3,2,1,0:T(8,128)(2,1)} fusion(bf16[8,4,128,128]{3,2,1,0:T(8,128)(2,1)} %get-tuple-element.11, s32[]{:T(128)S(6)} %select_n.3, bf16[4,128,128]{2,1,0:T(8,128)(2,1)S(1)} %collective-permute-done.4), kind=kLoop, calls=%fused_computation | loop fusion | bytes 262148 | tf_op jit(solution)/shard_map/dynamic_update_slice | solution.py:300
Async XLA Ops:
  1.3 30.8 %collective-permute-start.3 = (bf16[34,128,128]{2,1,0:T(8,128)(2,1)S(1)}, bf16[34,128,128]{2,1,0:T(8,128)(2,1)S(1)}, u32[]{:S(2)}, u32[]{:S(2)}) collective-permute-start(bf16[34,128,128]{2,1,0:T(8,128)(2,1)S(1)} %get-tuple-element.10), channel_id=1, source_target_pairs={{0,1},{1,2},{2,3},{3,4},{4,5},{5,6},{6,7},{16,17},{17,18},{18,19},... | collective-permute-start | bytes 3342344 | tf_op jit(solution)/shard_map/ppermute | solution.py:293
  6.2 3.4 %collective-permute-start = (bf16[8,16,128]{2,1,0:T(8,128)(2,1)S(1)}, bf16[8,16,128]{2,1,0:T(8,128)(2,1)S(1)}, u32[]{:S(2)}, u32[]{:S(2)}) collective-permute-start(bf16[8,16,128]{2,1,0:T(8,128)(2,1)S(1)} %get-tuple-element.9.refs_0_), channel_id=1, source_target_pairs={{0,8},{8,16},{16,24},{24,0},{1,9},{9,17},{17,25},{25,1},{2,10},{10... | collective-permute-start | bytes 98312 | tf_op jit(solution)/shard_map/ppermute | solution.py:30
  6.3 4.0 %collective-permute-start.1 = (bf16[8,16,128]{2,1,0:T(8,128)(2,1)S(1)}, bf16[8,16,128]{2,1,0:T(8,128)(2,1)S(1)}, u32[]{:S(2)}, u32[]{:S(2)}) collective-permute-start(bf16[8,16,128]{2,1,0:T(8,128)(2,1)S(1)} %get-tuple-element.9.refs_0_), channel_id=1, source_target_pairs={{0,16},{8,24},{16,0},{24,8},{1,17},{9,25},{17,1},{25,9},{2,18},{10... | collective-permute-start | bytes 98312 | tf_op jit(solution)/shard_map/ppermute | solution.py:30
  7.9 3.0 %collective-permute-start.2 = (bf16[8,16,128]{2,1,0:T(8,128)(2,1)S(1)}, bf16[8,16,128]{2,1,0:T(8,128)(2,1)S(1)}, u32[]{:S(2)}, u32[]{:S(2)}) collective-permute-start(bf16[8,16,128]{2,1,0:T(8,128)(2,1)S(1)} %get-tuple-element.9.refs_0_), channel_id=1, source_target_pairs={{0,24},{8,0},{16,8},{24,16},{1,25},{9,1},{17,9},{25,17},{2,26},{10... | collective-permute-start | bytes 98312 | tf_op jit(solution)/shard_map/ppermute | solution.py:30
  40.7 1.7 %collective-permute-start.4 = (bf16[4,128,128]{2,1,0:T(8,128)(2,1)S(1)}, bf16[4,128,128]{2,1,0:T(8,128)(2,1)S(1)}, u32[]{:S(2)}, u32[]{:S(2)}) collective-permute-start(bf16[4,128,128]{2,1,0:T(8,128)(2,1)S(1)} %get-tuple-element.12), channel_id=1, source_target_pairs={{0,8},{8,0},{16,24},{24,16},{1,9},{9,1},{17,25},{25,17},{2,10},{10... | collective-permute-start | bytes 393224 | tf_op jit(solution)/shard_map/ppermute | solution.py:299

commit v5 on v4

--- a/solution.py
+++ b/solution.py
@@ -26,7 +26,10 @@
 
 def gathered(mine, axis):
     count = lax.axis_size(axis)
-    turns = [[(m, (m + turn) % count) for m in range(count)] for turn in range(1, count)]
+    paired = count & (count - 1) == 0
+    turns = [
+        [(m, m ^ turn if paired else (m + turn) % count) for m in range(count)] for turn in range(1, count)
+    ]
     return [mine, *(lax.ppermute(mine, axis, pairs) for pairs in turns)]
 
 

time: 43.2 us -> 43.3 us (level)
  waiting for transfers between devices: 2.59 us -> 4.25 us
  starting transfers between devices: 8.62 us -> 7.08 us
    ppermute x3, waiting for transfers between devices: 1.6 us -> 3.07 us  [gathered(): return [mine, *(lax.ppermute(mine, axis, pairs) for pairs in turns)]]
    ppermute x3, starting transfers between devices: 3.03 us -> 1.93 us  [gathered(): return [mine, *(lax.ppermute(mine, axis, pairs) for pairs in turns)]]
    ppermute x1, starting transfers between devices: 0.67 us -> 0.23 us  [body(): passed = lax.ppermute(passed, 'mpo', [(m, m ^ 1) for m in range(groups)])]
  transfers between devices with their start and end apart: 5 -> 5, of which waited for: 4 -> 3; matrix products, arithmetic and copies ran while one was open for 0% -> 0% of each run, Pallas kernels for 49% -> 49%
where the time goes in v5:
time: 43.3 us; the launch traced here: 43.1 us
  Pallas kernels  31.1 us (72%)
  starting transfers between devices  7.08 us (16%)
  waiting for transfers between devices  4.25 us (10%)
  local copies, waits for them, and re-layouts  0.67 us (2%)
    pallas_call x2, Pallas kernels, apply_blocks(): pl.pallas_call(functools.partial(block_kernel, edge, count, own, total),...  29.8 us
    ppermute x1, starting transfers between devices, body(): halo = lax.ppermute(sent, ('mpo', 'blk'), up + down)  4.91 us
    ppermute x3, waiting for transfers between devices, gathered(): return [mine, *(lax.ppermute(mine, axis, pairs) for pairs in turns)]  3.07 us
    ppermute x3, starting transfers between devices, gathered(): return [mine, *(lax.ppermute(mine, axis, pairs) for pairs in turns)]  1.93 us
    pallas_call x1, Pallas kernels, ready(): pl.pallas_call(ready_kernel, out_shape=[pltpu.VMEM((terms, states, LANES)...  1.29 us
    ppermute x1, waiting for transfers between devices, body(): passed = lax.ppermute(passed, 'mpo', [(m, m ^ 1) for m in range(groups)])  1.18 us
  transfers between devices with their start and end apart: 5, of which 3 were waited for; matrix products, arithmetic and copies ran while one was open for 0% of the time, Pallas kernels for 49%

profile of v5, /device:TPU:0, one launch (start us, length us, event | category | flops | bytes accessed | tf_op | source)
XLA Modules:
  0.0 43.1 jit_solution(10539585087900351395)
XLA Ops:
  0.0 1.3 %ready.1 = (bf16[8,16,128]{2,1,0:T(8,128)(2,1)S(1)}, bf16[34,128,128]{2,1,0:T(8,128)(2,1)S(1)}) custom-call(s32[8]{0:T(128)} %left_hbm.1, s32[8]{0:T(128)} %right_hbm.1, bf16[8,16,16]{2,1,0:T(8,128)(2,1)} %terms_hbm.1, bf16[34,8,128,128]{3,2,1,0:T(8,128)(2,1)} %refs_10_.1), custom_call_target="tpu_custom_call" | custom-call | tf_op jit(solution)/shard_map/ready/pallas_call | solution.py:71
  1.3 4.9 %collective-permute-start.3 = (bf16[34,128,128]{2,1,0:T(8,128)(2,1)S(1)}, bf16[34,128,128]{2,1,0:T(8,128)(2,1)S(1)}, u32[]{:S(2)}, u32[]{:S(2)}) collective-permute-start(bf16[34,128,128]{2,1,0:T(8,128)(2,1)S(1)} %get-tuple-element.10), channel_id=1, source_target_pairs={{0,1},{1,2},{2,3},{3,4},{4,5},{5,6},{6,7},{16,17},{17,18},{18,19},... | collective-permute-start | bytes 3342344 | tf_op jit(solution)/shard_map/ppermute | solution.py:296
  6.2 0.1 collective-permute-start
  6.3 1.6 %collective-permute-start.1 = (bf16[8,16,128]{2,1,0:T(8,128)(2,1)S(1)}, bf16[8,16,128]{2,1,0:T(8,128)(2,1)S(1)}, u32[]{:S(2)}, u32[]{:S(2)}) collective-permute-start(bf16[8,16,128]{2,1,0:T(8,128)(2,1)S(1)} %get-tuple-element.9.refs_0_), channel_id=1, source_target_pairs={{0,16},{8,24},{16,0},{24,8},{1,17},{9,25},{17,1},{25,9},{2,18},{10... | collective-permute-start | bytes 98312 | tf_op jit(solution)/shard_map/ppermute | solution.py:33
  7.9 0.3 collective-permute-start.2
  8.2 0.0 collective-permute-done.refs_1_
  8.2 2.1 %collective-permute-done.1.refs_2_ = bf16[8,16,128]{2,1,0:T(8,128)(2,1)S(1)} collective-permute-done((bf16[8,16,128]{2,1,0:T(8,128)(2,1)S(1)}, bf16[8,16,128]{2,1,0:T(8,128)(2,1)S(1)}, u32[]{:S(2)}, u32[]{:S(2)}) %collective-permute-start.1) | collective-permute-done | bytes 32800 | tf_op jit(solution)/shard_map/ppermute | solution.py:33
  10.3 0.9 %collective-permute-done.2.refs_3_ = bf16[8,16,128]{2,1,0:T(8,128)(2,1)S(1)} collective-permute-done((bf16[8,16,128]{2,1,0:T(8,128)(2,1)S(1)}, bf16[8,16,128]{2,1,0:T(8,128)(2,1)S(1)}, u32[]{:S(2)}, u32[]{:S(2)}) %collective-permute-start.2) | collective-permute-done | bytes 32800 | tf_op jit(solution)/shard_map/ppermute | solution.py:33
  11.2 21.3 %inner_blocks.1.refs_6_ = bf16[8,4,128,128]{3,2,1,0:T(8,128)(2,1)} custom-call(bf16[8,16,128]{2,1,0:T(8,128)(2,1)S(1)} %get-tuple-element.9.refs_0_, bf16[8,16,128]{2,1,0:T(8,128)(2,1)S(1)} %collective-permute-done.refs_1_, bf16[8,16,128]{2,1,0:T(8,128)(2,1)S(1)} %collective-permute-done.1.refs_2_, bf16[8,16,128]{2,1,0:T(8,128)(2,1)S(1)} %collective-permute-done.2.refs_3_, ...), custom_call_target="tpu_custom_call" | custom-call | tf_op jit(solution)/shard_map/inner_blocks/pallas_call | solution.py:267
  32.5 0.0 collective-permute-done.3.refs_7_
  32.5 8.5 %edge_block.1 = (bf16[8,4,128,128]{3,2,1,0:T(8,128)(2,1)}, bf16[4,128,128]{2,1,0:T(8,128)(2,1)S(1)}) custom-call(bf16[8,16,128]{2,1,0:T(8,128)(2,1)S(1)} %get-tuple-element.9.refs_0_, bf16[8,16,128]{2,1,0:T(8,128)(2,1)S(1)} %collective-permute-done.refs_1_, bf16[8,16,128]{2,1,0:T(8,128)(2,1)S(1)} %collective-permute-done.1.refs_2_, ...), custom_call_target="tpu_custom_call", output_to_operand_aliasing={{0}: (6, {})} | custom-call | tf_op jit(solution)/shard_map/edge_block/pallas_call | solution.py:267
  41.0 0.2 collective-permute-start.4
  41.3 1.2 %collective-permute-done.4 = bf16[4,128,128]{2,1,0:T(8,128)(2,1)S(1)} collective-permute-done((bf16[4,128,128]{2,1,0:T(8,128)(2,1)S(1)}, bf16[4,128,128]{2,1,0:T(8,128)(2,1)S(1)}, u32[]{:S(2)}, u32[]{:S(2)}) %collective-permute-start.4) | collective-permute-done | bytes 131104 | tf_op jit(solution)/shard_map/ppermute | solution.py:302
  42.4 0.7 %bitcast_dynamic-update-slice_fusion = bf16[8,4,128,128]{3,2,1,0:T(8,128)(2,1)} fusion(bf16[8,4,128,128]{3,2,1,0:T(8,128)(2,1)} %get-tuple-element.11, s32[]{:T(128)S(6)} %select_n.3, bf16[4,128,128]{2,1,0:T(8,128)(2,1)S(1)} %collective-permute-done.4), kind=kLoop, calls=%fused_computation | loop fusion | bytes 262148 | tf_op jit(solution)/shard_map/dynamic_update_slice | solution.py:303
Async XLA Ops:
  1.3 31.2 %collective-permute-start.3 = (bf16[34,128,128]{2,1,0:T(8,128)(2,1)S(1)}, bf16[34,128,128]{2,1,0:T(8,128)(2,1)S(1)}, u32[]{:S(2)}, u32[]{:S(2)}) collective-permute-start(bf16[34,128,128]{2,1,0:T(8,128)(2,1)S(1)} %get-tuple-element.10), channel_id=1, source_target_pairs={{0,1},{1,2},{2,3},{3,4},{4,5},{5,6},{6,7},{16,17},{17,18},{18,19},... | collective-permute-start | bytes 3342344 | tf_op jit(solution)/shard_map/ppermute | solution.py:296
  6.2 1.9 %collective-permute-start = (bf16[8,16,128]{2,1,0:T(8,128)(2,1)S(1)}, bf16[8,16,128]{2,1,0:T(8,128)(2,1)S(1)}, u32[]{:S(2)}, u32[]{:S(2)}) collective-permute-start(bf16[8,16,128]{2,1,0:T(8,128)(2,1)S(1)} %get-tuple-element.9.refs_0_), channel_id=1, source_target_pairs={{0,8},{8,0},{16,24},{24,16},{1,9},{9,1},{17,25},{25,17},{2,10},{10... | collective-permute-start | bytes 98312 | tf_op jit(solution)/shard_map/ppermute | solution.py:33
  6.3 4.0 %collective-permute-start.1 = (bf16[8,16,128]{2,1,0:T(8,128)(2,1)S(1)}, bf16[8,16,128]{2,1,0:T(8,128)(2,1)S(1)}, u32[]{:S(2)}, u32[]{:S(2)}) collective-permute-start(bf16[8,16,128]{2,1,0:T(8,128)(2,1)S(1)} %get-tuple-element.9.refs_0_), channel_id=1, source_target_pairs={{0,16},{8,24},{16,0},{24,8},{1,17},{9,25},{17,1},{25,9},{2,18},{10... | collective-permute-start | bytes 98312 | tf_op jit(solution)/shard_map/ppermute | solution.py:33
  7.9 3.3 %collective-permute-start.2 = (bf16[8,16,128]{2,1,0:T(8,128)(2,1)S(1)}, bf16[8,16,128]{2,1,0:T(8,128)(2,1)S(1)}, u32[]{:S(2)}, u32[]{:S(2)}) collective-permute-start(bf16[8,16,128]{2,1,0:T(8,128)(2,1)S(1)} %get-tuple-element.9.refs_0_), channel_id=1, source_target_pairs={{0,24},{8,16},{16,8},{24,0},{1,25},{9,17},{17,9},{25,1},{2,26},{10... | collective-permute-start | bytes 98312 | tf_op jit(solution)/shard_map/ppermute | solution.py:33
  41.0 1.4 %collective-permute-start.4 = (bf16[4,128,128]{2,1,0:T(8,128)(2,1)S(1)}, bf16[4,128,128]{2,1,0:T(8,128)(2,1)S(1)}, u32[]{:S(2)}, u32[]{:S(2)}) collective-permute-start(bf16[4,128,128]{2,1,0:T(8,128)(2,1)S(1)} %get-tuple-element.12), channel_id=1, source_target_pairs={{0,8},{8,0},{16,24},{24,16},{1,9},{9,1},{17,25},{25,17},{2,10},{10... | collective-permute-start | bytes 393224 | tf_op jit(solution)/shard_map/ppermute | solution.py:302
